TPU v7x, 512 devices: a whole 4x8x8 slice. The times are simulated.
512 devices in a mesh: seq: 128 (over y, x, z_hi), tp: 4 (over z_lo, core).
Axes of the slice: x: 4, y: 8, z: 8 (z_hi: 4, z_lo: 2; z = z_hi * 2 + z_lo), core: 2. Of those that a mesh axis runs over, the one named last changes fastest.
Arguments:
- targets: bfloat16 [131072, 2048], P('seq', 'tp'), may hold values from -6 to 6
- w_query: bfloat16 [2048, 1024], P(None, 'tp'), may hold values from -0.125 to 0.125
- w_gate: bfloat16 [2048, 1024], P(None, 'tp'), may hold values from -0.125 to 0.125
- norm_gain: float32 [1024], P('tp'), may hold values from 0.25 to 1.75
- hist_keys: bfloat16 [131072, 1024], P('seq', 'tp'), may hold values from -6 to 6
- hist_values: bfloat16 [131072, 1024], P('seq', 'tp')
- user_offset: int32 [2048], P('seq'), may hold values from 0 to 131071, as said below
- user_length: int32 [2048], P('seq'), may hold values from 16 to 2048
- target_user: int32 [131072], P('seq'), may hold values from 0 to 2047, as said below
Outputs:
- scored: bfloat16 [131072, 1024], P('seq', 'tp')
Inputs may be any that keep to these rules, and one draw needn't show every extreme that they name: `user_offset`: the users of seq index i are users i * 16 to (i + 1) * 16 - 1; each such user's offset lies in history positions i * 1024 to (i + 1) * 1024 - 1. A history may run past position 131071 and continue at position 0. `target_user`: target items of seq index i belong to users of seq index i.
All inputs are finite; a program needn't handle non-finite values.
Results may differ from a plain program's by a relative error of at most 0.0058.
Values may be sent and summed in bfloat16 or wider, within the bound.
No kernel may reach another device: no remote copies, remote signals or barrier semaphores. Data moves between devices by JAX's collectives and lax.ppermute only.
A program may use at most 64 MiB of HBM per device.

v0:
```python
import jax
import jax.numpy as jnp
from jax import lax
from jax.sharding import PartitionSpec as P

HDIM = 128
SPAN = 2
U_DEV = 16
HQ = 1024


def from_behind(array, axis, by):
    size = lax.axis_size(axis)
    return lax.ppermute(array, axis, [(i, (i + by) % size) for i in range(size)])


def body(
    targets,
    w_query,
    w_gate,
    norm_gain,
    hist_keys,
    hist_values,
    user_offset,
    user_length,
    target_user,
):
    tgt_rows = targets.shape[0]
    hist_rows = hist_keys.shape[0]
    local_width = w_query.shape[1]
    local_heads = local_width // HDIM
    scale = HDIM ** (-0.5)
    piece = lax.all_gather(targets, "tp", axis=1, tiled=True)
    query_sum = jnp.dot(piece, w_query, preferred_element_type=jnp.float32)
    gate_sum = jnp.dot(piece, w_gate, preferred_element_type=jnp.float32)
    query = query_sum.astype(jnp.bfloat16).reshape(tgt_rows, local_heads, HDIM)
    gate = jax.nn.silu(gate_sum)
    seq_index = lax.axis_index("seq")
    local_user = target_user - seq_index * U_DEV
    matches = local_user[:, None] == jnp.arange(U_DEV, dtype=jnp.int32)[None, :]
    start_of = jnp.sum(jnp.where(matches, user_offset[None, :] - seq_index * hist_rows, 0), axis=1)
    length_of = jnp.sum(jnp.where(matches, user_length[None, :], 0), axis=1)

    def attend(block_pair, which):
        keys = block_pair[0].reshape(hist_rows, local_heads, HDIM)
        values = block_pair[1].reshape(hist_rows, local_heads, HDIM)
        relative = (
            which * hist_rows + jnp.arange(hist_rows, dtype=jnp.int32)[None, :] - start_of[:, None]
        )
        inside = (relative >= 0) & (relative < length_of[:, None])
        scores = jnp.einsum("thd,phd->thp", query, keys, preferred_element_type=jnp.float32) * scale
        weight = jnp.where(inside[:, None, :], jax.nn.silu(scores), 0.0).astype(jnp.bfloat16)
        mixed = jnp.einsum("thp,phd->thd", weight, values, preferred_element_type=jnp.float32)
        return mixed.reshape(tgt_rows, local_width)

    own_pair = (hist_keys, hist_values)
    attended = attend(own_pair, 0)
    current = own_pair
    for step in range(SPAN):
        current = from_behind((current[0], current[1]), "seq", -1)
        attended = attended + attend(current, step + 1)
    total_sum, total_square = lax.psum(
        (jnp.sum(attended, axis=1), jnp.sum(attended * attended, axis=1)), "tp"
    )
    mean = total_sum / HQ
    var = total_square / HQ - mean * mean
    normed = (attended - mean[:, None]) / jnp.sqrt(var[:, None] + 1e-05)
    return (normed * norm_gain[None, :] * gate).astype(jnp.bfloat16)


def solution(mesh):
    return jax.shard_map(
        body,
        mesh=mesh,
        in_specs=(
            P("seq", "tp"),
            P(None, "tp"),
            P(None, "tp"),
            P("tp"),
            P("seq", "tp"),
            P("seq", "tp"),
            P("seq"),
            P("seq"),
            P("seq"),
        ),
        out_specs=P("seq", "tp"),
        check_vma=False,
    )
```

profile of v0, /device:TPU:1, one launch (start us, length us, event | category | flops | bytes accessed | tf_op | source)
XLA Modules:
  0.0 190.0 jit_solution(14452313405230123794)
XLA Ops:
  6.5 0.0 copy-start
  6.5 0.0 all-gather.2.cloned.1.call-start
  6.5 0.7 all-gather.2.cloned.1.call-update
  7.3 2.0 %copy.32 = bf16[1024,256]{0,1:T(8,128)(2,1)} copy(bf16[1024,256]{1,0:T(8,128)(2,1)} %param.13) | data formatting | bytes 1048576 | tf_op args[4]
  9.3 16.6 %collective-permute-start = (bf16[1024,256]{0,1:T(8,128)(2,1)}, bf16[1024,256]{0,1:T(8,128)(2,1)}, u32[]{:S(2)}, u32[]{:S(2)}) collective-permute-start(bf16[1024,256]{0,1:T(8,128)(2,1)} %copy.32), channel_id=1, source_target_pairs={{0,508},{4,0},{8,4},{12,8},{16,12},{20,16},{24,20},{28,24},{32,28}... | collective-permute-start | bytes 1572872 | tf_op jit(solution)/shard_map/ppermute | solution.py:14
  25.9 2.2 %collective-permute-start.1 = (bf16[1024,256]{1,0:T(8,128)(2,1)}, bf16[1024,256]{1,0:T(8,128)(2,1)}, u32[]{:S(2)}, u32[]{:S(2)}) collective-permute-start(bf16[1024,256]{1,0:T(8,128)(2,1)} %param.14), channel_id=1, source_target_pairs={{0,508},{4,0},{8,4},{12,8},{16,12},{20,16},{24,20},{28,24},{32,28}... | collective-permute-start | bytes 1572872 | tf_op jit(solution)/shard_map/ppermute | solution.py:14
  28.1 2.1 %copy.45 = bf16[1024,256]{0,1:T(8,128)(2,1)} copy(bf16[1024,256]{1,0:T(8,128)(2,1)} %param.14) | data formatting | bytes 1048576 | tf_op jit(solution)/shard_map/reshape | solution.py:46
  30.1 0.7 broadcast_subtract_fusion.1
  30.8 0.7 broadcast_subtract_fusion
  31.5 0.8 select_reduce_fusion.1
  32.2 33.3 %collective-permute-done.1 = bf16[1024,256]{1,0:T(8,128)(2,1)} collective-permute-done((bf16[1024,256]{1,0:T(8,128)(2,1)}, bf16[1024,256]{1,0:T(8,128)(2,1)}, u32[]{:S(2)}, u32[]{:S(2)}) %collective-permute-start.1) | collective-permute-done | bytes 524320 | tf_op jit(solution)/shard_map/ppermute | solution.py:14
  65.6 12.3 %collective-permute-start.3 = (bf16[1024,256]{1,0:T(8,128)(2,1)}, bf16[1024,256]{1,0:T(8,128)(2,1)}, u32[]{:S(2)}, u32[]{:S(2)}) collective-permute-start(bf16[1024,256]{1,0:T(8,128)(2,1)} %collective-permute-done.1), channel_id=1, source_target_pairs={{0,508},{4,0},{8,4},{12,8},{16,12},{20,16},{24,20},{28,24},{32,28}... | collective-permute-start | bytes 1572872 | tf_op jit(solution)/shard_map/ppermute | solution.py:14
  77.9 4.5 %fusion.19 = (pred[1024,1024]{1,0:T(8,128)(4,1)S(1)}, pred[1024,1024]{1,0:T(8,128)(4,1)S(1)}, pred[1024,1024]{1,0:T(8,128)(4,1)}) fusion(s32[1024]{0:T(1024)S(1)} %get-tuple-element.17, s32[1024]{0:T(1024)S(1)} %get-tuple-element.8, s32[1024]{0:T(1024)S(1)} %get-tuple-element.7, s32[1024]{0:T(1024)S(1)} %get-tuple-element.18), kind=kLoop, calls=%fused_computation.30 | loop fusion | flops 12582912 | bytes 3162112 | tf_op jit(solution)/shard_map/and | solution.py:50
  82.4 2.1 %copy.35 = bf16[1024,256]{0,1:T(8,128)(2,1)} copy(bf16[1024,256]{1,0:T(8,128)(2,1)} %collective-permute-done.1) | data formatting | bytes 1048576 | tf_op jit(solution)/shard_map/ppermute | solution.py:14
  84.5 0.0 collective-permute-done
  84.5 2.1 %collective-permute-start.2 = (bf16[1024,256]{0,1:T(8,128)(2,1)}, bf16[1024,256]{0,1:T(8,128)(2,1)}, u32[]{:S(2)}, u32[]{:S(2)}) collective-permute-start(bf16[1024,256]{0,1:T(8,128)(2,1)} %collective-permute-done), channel_id=1, source_target_pairs={{0,508},{4,0},{8,4},{12,8},{16,12},{20,16},{24,20},{28,24},{32,28}... | collective-permute-start | bytes 1572872 | tf_op jit(solution)/shard_map/ppermute | solution.py:14
  86.6 0.0 collective-permute-done.3
  86.6 2.1 %copy.38 = bf16[1024,256]{0,1:T(8,128)(2,1)} copy(bf16[1024,256]{1,0:T(8,128)(2,1)} %collective-permute-done.3) | data formatting | bytes 1048576 | tf_op jit(solution)/shard_map/ppermute | solution.py:14
  88.7 59.3 %all-gather.2.cloned.1.call-done = bf16[1024,2048]{1,0:T(8,128)(2,1)} async-done(((bf16[1024,512]{1,0:T(8,128)(2,1)}), bf16[1024,2048]{1,0:T(8,128)(2,1)}) %all-gather.2.cloned.1.call-update) | async-done | bytes 4194320 | tf_op jit(solution)/shard_map/all_gather | solution.py:33
  147.9 0.0 copy-done
  147.9 4.3 %convolution_convert_fusion = bf16[1024,256]{0,1:T(8,128)(2,1)} fusion(bf16[1024,2048]{1,0:T(8,128)(2,1)} %all-gather.2.cloned.1.call-done, bf16[2048,256]{1,0:T(8,128)(2,1)S(1)} %copy-done), kind=kOutput, calls=%fused_computation.39 | convolution fusion | flops 1074003968 | bytes 5767168 | tf_op jit(solution)/shard_map/dot_general | solution.py:34
  152.2 6.9 %fusion.24 = f32[2,1024,128]{1,2,0:T(8,128)} fusion(bf16[1024,2,128]{0,2,1:T(8,128)(2,1)} %bitcast.85, pred[1024,1024]{1,0:T(8,128)(4,1)} %get-tuple-element.13, bf16[1024,2,128]{0,2,1:T(8,128)(2,1)} %bitcast.88, bf16[1024,256]{1,0:T(8,128)(2,1)} %param.13), kind=kOutput, calls=%fused_computation.33 | convolution fusion | flops 1088421888 | bytes 3670016 | tf_op jit(solution)/shard_map/thp,phd->thd/dot_general | solution.py:53
  159.2 6.9 %fusion.32 = f32[2,1024,128]{1,2,0:T(8,128)} fusion(f32[2,1024,128]{1,2,0:T(8,128)} %fusion.24, bf16[1024,2,128]{0,2,1:T(8,128)(2,1)} %bitcast.86, pred[1024,1024]{1,0:T(8,128)(4,1)S(1)} %get-tuple-element.12, bf16[1024,2,128]{0,2,1:T(8,128)(2,1)} %bitcast.89, bf16[1024,2,128]{0,2,1:T(8,128)(2,1)} %bitcast.3), kind=kOutput, calls=%fused_computation.37 | convolution fusion | flops 1088684032 | bytes 4718592 | tf_op jit(solution)/shard_map/thp,phd->thd/dot_general | solution.py:53
  166.1 0.0 collective-permute-done.2
  166.1 6.2 %fusion.51 = (f32[1024]{0:T(1024)S(1)}, f32[1024]{0:T(1024)S(1)}, f32[2,1024,128]{1,2,0:T(8,128)S(1)}) fusion(f32[2,1024,128]{1,2,0:T(8,128)} %fusion.32, bf16[1024,2,128]{0,2,1:T(8,128)(2,1)} %bitcast.87, pred[1024,1024]{1,0:T(8,128)(4,1)S(1)} %get-tuple-element.11, bf16[1024,2,128]{0,2,1:T(8,128)(2,1)} %bitcast.90, bf16[1024,2,128]{0,2,1:T(8,128)(2,1)} %bitcast.6), kind=kOutput, calls=%fused_computation.62 | convolution fusion | flops 1089468416 | bytes 4726784 | tf_op jit(solution)/shard_map/thp,phd->thd/dot_general | solution.py:53
  172.3 0.3 copy.39
  172.7 0.0 copy-start.1
  172.7 5.5 %all-reduce = (f32[1024]{0:T(1024)S(1)}, f32[1024]{0:T(1024)S(1)}) all-reduce(f32[1024]{0:T(1024)S(1)} %get-tuple-element.6, f32[1024]{0:T(1024)S(1)} %get-tuple-element.5), channel_id=1, replica_groups=mesh['seq'=128,'tp'=4] {'tp'}, use_global_device_ids=true, to_apply=%region_5.6 | all-reduce | flops 2048 | bytes 16384 | tf_op jit(solution)/shard_map/psum | solution.py:62
  178.2 3.7 %fusion.52 = f32[1024,256]{1,0:T(8,128)S(1)} fusion(bf16[1024,2048]{1,0:T(8,128)(2,1)} %all-gather.2.cloned.1.call-done, bf16[2048,256]{1,0:T(8,128)(2,1)} %param.11), kind=kOutput, calls=%fused_computation.63 | convolution fusion | flops 1073741824 | bytes 6291456 | tf_op jit(solution)/shard_map/dot_general | solution.py:35
  181.9 0.0 copy-done.1
  181.9 1.2 multiply_convert_fusion
  (2 shorter events, 0.0 us)
Async XLA Ops:
  6.5 141.4 %copy-start = (bf16[2048,256]{1,0:T(8,128)(2,1)S(1)}, bf16[2048,256]{1,0:T(8,128)(2,1)}, u32[]{:S(2)}) copy-start(bf16[2048,256]{1,0:T(8,128)(2,1)} %param.10) | copy-start | bytes 3145732
  6.5 141.4 %all-gather.2.cloned.1.call-start = ((), (), s32[]{:S(2)}) async-start(), calls=%async_computation | async-start | bytes 5242880 | tf_op jit(solution)/shard_map/all_gather | solution.py:33
  9.3 75.2 %collective-permute-start = (bf16[1024,256]{0,1:T(8,128)(2,1)}, bf16[1024,256]{0,1:T(8,128)(2,1)}, u32[]{:S(2)}, u32[]{:S(2)}) collective-permute-start(bf16[1024,256]{0,1:T(8,128)(2,1)} %copy.32), channel_id=1, source_target_pairs={{0,508},{4,0},{8,4},{12,8},{16,12},{20,16},{24,20},{28,24},{32,28}... | collective-permute-start | bytes 1572872 | tf_op jit(solution)/shard_map/ppermute | solution.py:14
  25.9 39.7 %collective-permute-start.1 = (bf16[1024,256]{1,0:T(8,128)(2,1)}, bf16[1024,256]{1,0:T(8,128)(2,1)}, u32[]{:S(2)}, u32[]{:S(2)}) collective-permute-start(bf16[1024,256]{1,0:T(8,128)(2,1)} %param.14), channel_id=1, source_target_pairs={{0,508},{4,0},{8,4},{12,8},{16,12},{20,16},{24,20},{28,24},{32,28}... | collective-permute-start | bytes 1572872 | tf_op jit(solution)/shard_map/ppermute | solution.py:14
  65.6 21.0 %collective-permute-start.3 = (bf16[1024,256]{1,0:T(8,128)(2,1)}, bf16[1024,256]{1,0:T(8,128)(2,1)}, u32[]{:S(2)}, u32[]{:S(2)}) collective-permute-start(bf16[1024,256]{1,0:T(8,128)(2,1)} %collective-permute-done.1), channel_id=1, source_target_pairs={{0,508},{4,0},{8,4},{12,8},{16,12},{20,16},{24,20},{28,24},{32,28}... | collective-permute-start | bytes 1572872 | tf_op jit(solution)/shard_map/ppermute | solution.py:14
  84.5 81.6 %collective-permute-start.2 = (bf16[1024,256]{0,1:T(8,128)(2,1)}, bf16[1024,256]{0,1:T(8,128)(2,1)}, u32[]{:S(2)}, u32[]{:S(2)}) collective-permute-start(bf16[1024,256]{0,1:T(8,128)(2,1)} %collective-permute-done), channel_id=1, source_target_pairs={{0,508},{4,0},{8,4},{12,8},{16,12},{20,16},{24,20},{28,24},{32,28}... | collective-permute-start | bytes 1572872 | tf_op jit(solution)/shard_map/ppermute | solution.py:14
  172.7 9.3 %copy-start.1 = (f32[256]{0:T(256)S(1)}, f32[256]{0:T(256)}, u32[]{:S(2)}) copy-start(f32[256]{0:T(256)} %param.12) | copy-start | bytes 3076
Sparse Core Ops, SparseCore 0:
  9.5 138.4 all-gather.1
where the time goes:
time: 191 us; the launch traced here: 190 us
  waiting for transfers between devices  93.3 us (49%)
  starting transfers between devices  33.2 us (17%)
  matrix products  28.1 us (15%)
  between operations  13.5 us (7%)
  local copies, waits for them, and re-layouts  8.59 us (4%)
  other arithmetic  7.86 us (4%)
  blocking collectives  5.5 us (3%)
    all_gather x1, waiting for transfers between devices, body(): piece = lax.all_gather(targets, 'tp', axis=1, tiled=True)  59.3 us
    ppermute x4, waiting for transfers between devices, from_behind(): lax.ppermute(array, axis, [(i, (i + by) % size) for i in range(size)])  33.3 us
    ppermute x4, starting transfers between devices, from_behind(): lax.ppermute(array, axis, [(i, (i + by) % size) for i in range(size)])  33.2 us
    dot_general x3, matrix products, attend(): jnp.einsum('thp,phd->thd', weight, values, preferred_element_type=jnp.flo...  20.1 us
    psum x1, blocking collectives, body(): lax.psum((jnp.sum(attended, axis=1), jnp.sum(attended * attended, axis=1)...  5.5 us
    and x1, other arithmetic, attend(): inside = (relative >= 0) & (relative < length_of[:, None])  4.51 us
    dot_general x1, matrix products, body(): query_sum = jnp.dot(piece, w_query, preferred_element_type=jnp.float32)  4.33 us
    ppermute x2, local copies, waits for them, and re-layouts, from_behind(): lax.ppermute(array, axis, [(i, (i + by) % size) for i in range(size)])  4.14 us
  transfers between devices with their start and end apart: 5, of which 2 were waited for; matrix products, arithmetic and copies ran while one was open for 17% of the time, Pallas kernels for 0%

commit v1 on v0

v1 whole, which is shorter than its diff:
```python
import functools

import jax
import jax.numpy as jnp
from jax import lax
from jax.experimental import pallas as pl
from jax.experimental.pallas import tpu as pltpu
from jax.sharding import PartitionSpec as P

HDIM = 128
U_DEV = 16
HQ = 1024
Z_HI = 4
LANES = 128
DOWN_ROWS = 640
VMEM = pl.BlockSpec(memory_space=pltpu.VMEM)
SMEM = pl.BlockSpec(memory_space=pltpu.SMEM)
PARAMS = pltpu.CompilerParams(vmem_limit_bytes=40 * 2**20)


def ring_perms(n_seq):
    down = [(i, (i - 1) % n_seq) for i in range(n_seq)]
    up = []
    for stage in range(3):
        pairs = []
        for i in range(n_seq):
            column, z = divmod(i, Z_HI)
            origin = (z - stage) % Z_HI
            shift = 0
            if stage == 1 and origin == 0:
                shift = -1
            if stage == 1 and origin == 1:
                shift = -1
            if stage == 2 and origin == 1:
                shift = 1
            target = (column + shift) % (n_seq // Z_HI) * Z_HI + (z + 1) % Z_HI
            pairs.append((i, target))
        up.append(pairs)
    return down, up


def windows_kernel(seq_ref, offset_ref, length_ref, user_ref, start_ref, end_ref):
    first_user = seq_ref[0] * U_DEV
    first_row = seq_ref[0] * seq_ref[1]
    user = user_ref[...] - first_user
    start = jnp.zeros_like(user)
    end = jnp.zeros_like(user)
    for u in range(U_DEV):
        mine = user == u
        low = offset_ref[u] - first_row
        start = jnp.where(mine, low, start)
        end = jnp.where(mine, low + length_ref[u], end)
    for group in range(user.shape[0]):
        rows = slice(group * LANES, (group + 1) * LANES)
        start_ref[rows, :] = jnp.broadcast_to(start[group : group + 1], (LANES, LANES)).T
        end_ref[rows, :] = jnp.broadcast_to(end[group : group + 1], (LANES, LANES)).T


def windows(seq_info, user_offset, user_length, target_user):
    rows = target_user.shape[0]
    wide = jax.ShapeDtypeStruct((rows, LANES), jnp.int32)
    return pl.pallas_call(
        windows_kernel,
        out_shape=(wide, wide),
        in_specs=[SMEM, SMEM, SMEM, VMEM],
        out_specs=(VMEM, VMEM),
        compiler_params=PARAMS,
    )(seq_info, user_offset, user_length, target_user.reshape(rows // LANES, LANES))


def project_kernel(order_ref, a_ref, b_ref, wqa, wqb, wga, wgb, *refs, last):
    a, b = a_ref[...], b_ref[...]
    dot = functools.partial(jnp.dot, preferred_element_type=jnp.float32)
    query = dot(a, wqa[...]) + dot(b, wqb[...])
    gate = dot(a, wga[...]) + dot(b, wgb[...])
    width = query.shape[1]
    if last:
        partial_ref, query_ref, gate_ref = refs
        query_ref[...] = (query + partial_ref[:, :width]).astype(jnp.bfloat16)
        gate_ref[...] = jax.nn.silu(gate + partial_ref[:, width:])
    else:
        (partial_ref,) = refs
        partial_ref[:, :width] = query
        partial_ref[:, width:] = gate


def project(order, a, b, w_query, w_gate, partial=None):
    rows, depth = a.shape
    width = w_query.shape[1]
    tile = 256
    feature = pl.BlockSpec((tile, depth), lambda i, order: (i, 0))
    first = pl.BlockSpec((depth, width), lambda i, order: (order[0], 0))
    second = pl.BlockSpec((depth, width), lambda i, order: (order[1], 0))
    sums = pl.BlockSpec((tile, 2 * width), lambda i, order: (i, 0))
    half = pl.BlockSpec((tile, width), lambda i, order: (i, 0))
    in_specs = [feature, feature, first, second, first, second]
    args = [a, b, w_query, w_query, w_gate, w_gate]
    if partial is None:
        out_specs = sums
        out_shape = jax.ShapeDtypeStruct((rows, 2 * width), jnp.float32)
    else:
        in_specs.append(sums)
        args.append(partial)
        out_specs = (half, half)
        out_shape = (
            jax.ShapeDtypeStruct((rows, width), jnp.bfloat16),
            jax.ShapeDtypeStruct((rows, width), jnp.float32),
        )
    return pl.pallas_call(
        functools.partial(project_kernel, last=partial is not None),
        out_shape=out_shape,
        grid_spec=pltpu.PrefetchScalarGridSpec(
            num_scalar_prefetch=1, grid=(rows // tile,), in_specs=in_specs, out_specs=out_specs
        ),
        compiler_params=PARAMS,
        cost_estimate=pl.CostEstimate(
            flops=8 * rows * depth * width, bytes_accessed=8 * rows * depth, transcendentals=0
        ),
    )(order, *args)


def weigh(query, keys, values, start, end, place, total):
    rows = query.shape[0]
    for at in range(0, keys.shape[0], 256):
        size = min(256, keys.shape[0] - at)
        scores = lax.dot_general(
            query, keys[at : at + size], (((1,), (1,)), ((), ())), preferred_element_type=jnp.float32
        )
        columns = []
        for lane in range(0, size, LANES):
            half = scores[:, lane : lane + LANES] * (0.5 * HDIM**-0.5)
            weight = half * jnp.tanh(half) + half
            position = lax.broadcasted_iota(jnp.int32, (rows, LANES), 1) + (place + at + lane)
            inside = position < end
            if start is not None:
                inside = inside & (position >= start)
            columns.append(jnp.where(inside, weight, 0.0).astype(jnp.bfloat16))
        total = total + jnp.dot(
            jnp.concatenate(columns, axis=1), values[at : at + size], preferred_element_type=jnp.float32
        )
    return total


def own_kernel(query_ref, start_ref, end_ref, key_ref, value_ref, out_ref):
    for head in range(query_ref.shape[1] // HDIM):
        cols = slice(head * HDIM, (head + 1) * HDIM)
        zero = jnp.zeros((query_ref.shape[0], HDIM), jnp.float32)
        out_ref[:, cols] = weigh(
            query_ref[:, cols], key_ref[:, cols], value_ref[:, cols], start_ref[...], end_ref[...], 0, zero
        )


def next_kernel(query_ref, end_ref, pair_ref, total_ref, out_ref, *stats, place):
    parts = []
    for head in range(query_ref.shape[1] // HDIM):
        cols = slice(head * HDIM, (head + 1) * HDIM)
        part = weigh(
            query_ref[:, cols], pair_ref[0, :, cols], pair_ref[1, :, cols], None, end_ref[...], place,
            total_ref[:, cols],
        )
        out_ref[:, cols] = part
        parts.append(part)
    if stats:
        (stats_ref,) = stats
        plain = functools.reduce(jnp.add, parts)
        square = functools.reduce(jnp.add, [part * part for part in parts])
        for group in range(plain.shape[0] // LANES):
            rows = slice(group * LANES, (group + 1) * LANES)
            stats_ref[0:1, rows] = jnp.sum(plain[rows].T, axis=0, keepdims=True)
            stats_ref[1:2, rows] = jnp.sum(square[rows].T, axis=0, keepdims=True)


def attend_cost(rows, history, width):
    return pl.CostEstimate(
        flops=4 * rows * history * width, bytes_accessed=8 * rows * width, transcendentals=rows * history * 2
    )


def attend_own(query, start, end, keys, values):
    return pl.pallas_call(
        own_kernel,
        out_shape=jax.ShapeDtypeStruct(query.shape, jnp.float32),
        in_specs=[VMEM] * 5,
        out_specs=VMEM,
        compiler_params=PARAMS,
        cost_estimate=attend_cost(query.shape[0], *keys.shape),
    )(query, start, end, keys, values)


def attend_next(query, end, pair, total, place, last=False):
    out_shape = [jax.ShapeDtypeStruct(query.shape, jnp.float32)]
    if last:
        out_shape.append(jax.ShapeDtypeStruct((2, query.shape[0]), jnp.float32))
    out = pl.pallas_call(
        functools.partial(next_kernel, place=place),
        out_shape=out_shape,
        in_specs=[VMEM] * 4,
        out_specs=[VMEM] * len(out_shape),
        input_output_aliases={3: 0},
        compiler_params=PARAMS,
        cost_estimate=attend_cost(query.shape[0], *pair.shape[1:]),
    )(query, end, pair, total)
    return out if last else out[0]


def body(
    targets,
    w_query,
    w_gate,
    norm_gain,
    hist_keys,
    hist_values,
    user_offset,
    user_length,
    target_user,
):
    hist_rows = hist_keys.shape[0]
    down, up = ring_perms(lax.axis_size("seq"))
    cut = DOWN_ROWS
    other_chip = [(0, 2), (2, 0), (1, 3), (3, 1)]
    other_core = [(0, 1), (1, 0), (2, 3), (3, 2)]

    pair_a = jnp.stack([hist_keys[:cut], hist_values[:cut]])
    pair_b = jnp.stack([hist_keys[cut:], hist_values[cut:]])
    far = lax.ppermute(targets, "tp", other_chip)
    next_a = lax.ppermute(pair_a, "seq", down)
    up_b = lax.ppermute(pair_b, "seq", up[0])
    near = lax.ppermute(targets, "tp", other_core)
    far_near = lax.ppermute(far, "tp", other_core)
    over_b = lax.ppermute(up_b, "seq", up[1])
    over_a = lax.ppermute(next_a, "seq", down)
    next_b = lax.ppermute(over_b, "seq", up[2])

    me = lax.axis_index("tp").astype(jnp.int32)
    seq_info = jnp.stack([lax.axis_index("seq").astype(jnp.int32), jnp.int32(hist_rows)])
    start, end = windows(seq_info, user_offset, user_length, target_user)
    partial = project(jnp.stack([me, me ^ 1]), targets, near, w_query, w_gate)
    query, gate = project(jnp.stack([me ^ 2, me ^ 3]), far, far_near, w_query, w_gate, partial)

    total = attend_own(query, start, end, hist_keys, hist_values)
    total = attend_next(query, end, next_a, total, hist_rows)
    total = attend_next(query, end, over_b, total, 2 * hist_rows + cut)
    total = attend_next(query, end, over_a, total, 2 * hist_rows)
    attended, stats = attend_next(query, end, next_b, total, hist_rows + cut, last=True)

    sums = lax.psum(stats, "tp") / HQ
    mean = sums[0]
    var = sums[1] - mean * mean
    normed = (attended - mean[:, None]) / jnp.sqrt(var[:, None] + 1e-05)
    return (normed * norm_gain[None, :] * gate).astype(jnp.bfloat16)


def solution(mesh):
    return jax.shard_map(
        body,
        mesh=mesh,
        in_specs=(
            P("seq", "tp"),
            P(None, "tp"),
            P(None, "tp"),
            P("tp"),
            P("seq", "tp"),
            P("seq", "tp"),
            P("seq"),
            P("seq"),
            P("seq"),
        ),
        out_specs=P("seq", "tp"),
        check_vma=False,
    )
```

time: 191 us -> 145 us (0.76)
  the two profiles are of different devices: /device:TPU:1 before, /device:TPU:186 now
where the time goes in v1:
time: 145 us; the launch traced here: 144 us
  waiting for transfers between devices  63 us (43%)
  starting transfers between devices  49.3 us (34%)
  Pallas kernels  21.2 us (15%)
  blocking collectives  5.86 us (4%)
  other arithmetic  2.34 us (2%)
  local copies, waits for them, and re-layouts  2.22 us (2%)
    ppermute x1, waiting for transfers between devices, body(): far = lax.ppermute(targets, 'tp', other_chip)  32.4 us
    ppermute x1, starting transfers between devices, body(): next_b = lax.ppermute(over_b, 'seq', up[2])  25.3 us
    ppermute x1, waiting for transfers between devices, body(): up_b = lax.ppermute(pair_b, 'seq', up[0])  23.7 us
    pallas_call x4, Pallas kernels, attend_next(): pl.pallas_call(functools.partial(next_kernel, place=place), out_shape=out...  8.93 us
    pallas_call x2, Pallas kernels, project(): pl.pallas_call(functools.partial(project_kernel, last=partial is not None...  7.86 us
    ppermute x1, starting transfers between devices, body(): up_b = lax.ppermute(pair_b, 'seq', up[0])  6.98 us
    ppermute x1, waiting for transfers between devices, body(): over_b = lax.ppermute(up_b, 'seq', up[1])  6.77 us
    psum x1, blocking collectives, body(): sums = lax.psum(stats, 'tp') / HQ  5.86 us
  transfers between devices with their start and end apart: 8, of which 3 were waited for; matrix products, arithmetic and copies ran while one was open for 2% of the time, Pallas kernels for 14%

profile of v1, /device:TPU:186, one launch (start us, length us, event | category | flops | bytes accessed | tf_op | source)
XLA Modules:
  0.0 144.1 jit_solution(13949735577855528609)
XLA Ops:
  0.0 0.0 copy-start.2
  0.0 0.0 copy-start.5
  0.0 0.0 copy-start.6
  0.0 0.0 copy-start.7
  0.0 0.0 copy-start
  0.0 0.0 copy-start.1
  0.0 4.5 %collective-permute-start = (bf16[1024,512]{1,0:T(8,128)(2,1)}, bf16[1024,512]{1,0:T(8,128)(2,1)}, u32[]{:S(2)}, u32[]{:S(2)}) collective-permute-start(bf16[1024,512]{1,0:T(8,128)(2,1)} %a_ref.1), channel_id=1, source_target_pairs={{0,2},{2,0},{1,3},{3,1},{4,6},{6,4},{5,7},{7,5},{8,10},{10,8},{9,1... | collective-permute-start | bytes 3145736 | tf_op jit(solution)/shard_map/ppermute | solution.py:225
  4.6 1.9 %collective-permute-start.2 = (bf16[1024,512]{1,0:T(8,128)(2,1)}, bf16[1024,512]{1,0:T(8,128)(2,1)}, u32[]{:S(2)}, u32[]{:S(2)}) collective-permute-start(bf16[1024,512]{1,0:T(8,128)(2,1)} %a_ref.1), channel_id=1, source_target_pairs={{0,1},{1,0},{2,3},{3,2},{4,5},{5,4},{6,7},{7,6},{8,9},{9,8},{10,11... | collective-permute-start | bytes 3145736 | tf_op jit(solution)/shard_map/ppermute | solution.py:228
  6.5 1.1 slice_bitcast_fusion
  7.6 0.9 pad_maximum_fusion
  8.6 1.9 %collective-permute-start.6 = (bf16[2,640,256]{2,1,0:T(8,128)(2,1)}, bf16[2,640,256]{2,1,0:T(8,128)(2,1)}, u32[]{:S(2)}, u32[]{:S(2)}) collective-permute-start(bf16[2,640,256]{2,1,0:T(8,128)(2,1)} %pad_maximum_fusion), channel_id=1, source_target_pairs={{0,508},{4,0},{8,4},{12,8},{16,12},{20,16},{24,20},{28,24},{32,28}... | collective-permute-start | bytes 1966088 | tf_op jit(solution)/shard_map/ppermute | solution.py:226
  10.5 32.4 %collective-permute-done.a_ref = bf16[1024,512]{1,0:T(8,128)(2,1)} collective-permute-done((bf16[1024,512]{1,0:T(8,128)(2,1)}, bf16[1024,512]{1,0:T(8,128)(2,1)}, u32[]{:S(2)}, u32[]{:S(2)}) %collective-permute-start) | collective-permute-done | bytes 1048608 | tf_op jit(solution)/shard_map/ppermute | solution.py:225
  42.9 1.9 %collective-permute-start.1 = (bf16[1024,512]{1,0:T(8,128)(2,1)}, bf16[1024,512]{1,0:T(8,128)(2,1)}, u32[]{:S(2)}, u32[]{:S(2)}) collective-permute-start(bf16[1024,512]{1,0:T(8,128)(2,1)} %collective-permute-done.a_ref), channel_id=1, source_target_pairs={{0,1},{1,0},{2,3},{3,2},{4,5},{5,4},{6,7},{7,6},{8,9},{9,8},{10,11... | collective-permute-start | bytes 3145736 | tf_op jit(solution)/shard_map/ppermute | solution.py:229
  44.8 1.1 slice_bitcast_fusion.2
  45.9 7.0 %collective-permute-start.3 = (bf16[2,384,256]{2,1,0:T(8,128)(2,1)S(1)}, bf16[2,384,256]{2,1,0:T(8,128)(2,1)}, u32[]{:S(2)}, u32[]{:S(2)}) collective-permute-start(bf16[2,384,256]{2,1,0:T(8,128)(2,1)S(1)} %pad_maximum_fusion.1), channel_id=1, source_target_pairs={{0,4},{4,8},{8,12},{12,0},{16,20},{20,24},{24,28},{28,16},{32,36},... | collective-permute-start | bytes 1179656 | tf_op jit(solution)/shard_map/ppermute | solution.py:227
  52.9 23.7 %collective-permute-done.3 = bf16[2,384,256]{2,1,0:T(8,128)(2,1)} collective-permute-done((bf16[2,384,256]{2,1,0:T(8,128)(2,1)S(1)}, bf16[2,384,256]{2,1,0:T(8,128)(2,1)}, u32[]{:S(2)}, u32[]{:S(2)}) %collective-permute-start.3) | collective-permute-done | bytes 393248 | tf_op jit(solution)/shard_map/ppermute | solution.py:227
  76.7 1.9 %collective-permute-start.4 = (bf16[2,384,256]{2,1,0:T(8,128)(2,1)}, bf16[2,384,256]{2,1,0:T(8,128)(2,1)S(1)}, u32[]{:S(2)}, u32[]{:S(2)}) collective-permute-start(bf16[2,384,256]{2,1,0:T(8,128)(2,1)} %collective-permute-done.3), channel_id=1, source_target_pairs={{0,4},{4,504},{8,508},{12,0},{16,20},{20,8},{24,12},{28,16},{32,36... | collective-permute-start | bytes 1179656 | tf_op jit(solution)/shard_map/ppermute | solution.py:230
  78.6 0.0 collective-permute-done.6.pair_ref
  78.6 4.8 %collective-permute-start.7 = (bf16[2,640,256]{2,1,0:T(8,128)(2,1)}, bf16[2,640,256]{2,1,0:T(8,128)(2,1)}, u32[]{:S(2)}, u32[]{:S(2)}) collective-permute-start(bf16[2,640,256]{2,1,0:T(8,128)(2,1)} %collective-permute-done.6.pair_ref), channel_id=1, source_target_pairs={{0,508},{4,0},{8,4},{12,8},{16,12},{20,16},{24,20},{28,24},{32,28}... | collective-permute-start | bytes 1966088 | tf_op jit(solution)/shard_map/ppermute | solution.py:231
  83.4 0.1 pad_add_fusion.2.seq_ref
  83.5 0.0 copy-done.5
  83.5 0.0 copy-done.6
  83.5 0.0 copy-done.7
  83.5 0.9 shard_map.93
  84.4 0.1 pad_add_fusion.1.order_ref
  84.5 0.1 pad_add_fusion.order_ref
  84.6 6.8 %collective-permute-done.4.pair_ref = bf16[2,384,256]{2,1,0:T(8,128)(2,1)S(1)} collective-permute-done((bf16[2,384,256]{2,1,0:T(8,128)(2,1)}, bf16[2,384,256]{2,1,0:T(8,128)(2,1)S(1)}, u32[]{:S(2)}, u32[]{:S(2)}) %collective-permute-start.4) | collective-permute-done | bytes 393248 | tf_op jit(solution)/shard_map/ppermute | solution.py:230
  91.3 25.3 %collective-permute-start.5 = (bf16[2,384,256]{2,1,0:T(8,128)(2,1)S(1)}, bf16[2,384,256]{2,1,0:T(8,128)(2,1)S(1)}, u32[]{:S(2)}, u32[]{:S(2)}) collective-permute-start(bf16[2,384,256]{2,1,0:T(8,128)(2,1)S(1)} %collective-permute-done.4.pair_ref), channel_id=1, source_target_pairs={{0,4},{4,8},{8,12},{12,16},{16,20},{20,24},{24,28},{28,32},{32,36}... | collective-permute-start | bytes 1179656 | tf_op jit(solution)/shard_map/ppermute | solution.py:232
  116.6 0.0 collective-permute-done.2.b_ref
  116.6 0.0 copy-done.2
  116.7 0.0 copy-done
  116.7 0.0 copy-done.1
  116.7 3.8 %shard_map.91.refs_0_ = f32[1024,512]{1,0:T(8,128)S(1)} custom-call(s32[2]{0:T(128)S(1)} %pad_add_fusion.1.order_ref, bf16[1024,512]{1,0:T(8,128)(2,1)S(1)} %copy-done.2, bf16[1024,512]{1,0:T(8,128)(2,1)} %collective-permute-done.2.b_ref, bf16[2048,256]{1,0:T(8,128)(2,1)S(1)} %copy-done, bf16[2048,256]{1,0:T(8,128)(2,1)S(1)} %copy-done, ...), custom_call_target="tpu_custom_call" | custom-call | flops 1073741824 | bytes 4194304 | tf_op jit(solution)/shard_map/pallas_call | solution.py:109
  120.5 0.0 copy-start.3
  120.5 0.0 copy-start.4
  120.5 0.0 collective-permute-done.1.b_ref
  120.5 4.0 %shard_map.92 = (bf16[1024,256]{1,0:T(8,128)(2,1)S(1)}, f32[1024,256]{1,0:T(8,128)S(1)}) custom-call(s32[2]{0:T(128)S(1)} %pad_add_fusion.order_ref, bf16[1024,512]{1,0:T(8,128)(2,1)} %collective-permute-done.a_ref, bf16[1024,512]{1,0:T(8,128)(2,1)} %collective-permute-done.1.b_ref, bf16[2048,256]{1,0:T(8,128)(2,1)S(1)} %copy-done, ...), custom_call_target="tpu_custom_call" | custom-call | flops 1073741824 | bytes 4194304 | tf_op jit(solution)/shard_map/pallas_call | solution.py:109
  124.6 0.0 copy-done.3
  124.6 0.0 copy-done.4
  124.6 3.5 %shard_map.94.total_ref = f32[1024,256]{1,0:T(8,128)S(1)} custom-call(bf16[1024,256]{1,0:T(8,128)(2,1)S(1)} %get-tuple-element.11.query_ref, s32[1024,128]{1,0:T(8,128)S(1)} %get-tuple-element.13.start_ref, s32[1024,128]{1,0:T(8,128)S(1)} %get-tuple-element.12.end_ref, bf16[1024,256]{1,0:T(8,128)(2,1)S(1)} %copy-done.4, bf16[1024,256]{1,0:T(8,128)(2,1)S(1)} %copy-done.3), custom_call_target="tpu_custom_call" | custom-call | flops 1073741824 | bytes 2097152 | tf_op jit(solution)/shard_map/pallas_call | solution.py:180
  128.1 3.0 %shard_map.95.total_ref = f32[1024,256]{1,0:T(8,128)S(1)} custom-call(bf16[1024,256]{1,0:T(8,128)(2,1)S(1)} %get-tuple-element.11.query_ref, s32[1024,128]{1,0:T(8,128)S(1)} %get-tuple-element.12.end_ref, bf16[2,640,256]{2,1,0:T(8,128)(2,1)} %collective-permute-done.6.pair_ref, f32[1024,256]{1,0:T(8,128)S(1)} %shard_map.94.total_ref), custom_call_target="tpu_custom_call", output_to_operand_aliasing={{}: (3, {})} | custom-call | flops 671088640 | bytes 2097152 | tf_op jit(solution)/shard_map/pallas_call | solution.py:194
  131.0 1.4 shard_map.96.total_ref
  132.4 0.0 collective-permute-done.7.pair_ref
  132.4 2.9 %shard_map.97.total_ref = f32[1024,256]{1,0:T(8,128)S(1)} custom-call(bf16[1024,256]{1,0:T(8,128)(2,1)S(1)} %get-tuple-element.11.query_ref, s32[1024,128]{1,0:T(8,128)S(1)} %get-tuple-element.12.end_ref, bf16[2,640,256]{2,1,0:T(8,128)(2,1)} %collective-permute-done.7.pair_ref, f32[1024,256]{1,0:T(8,128)S(1)} %shard_map.96.total_ref), custom_call_target="tpu_custom_call", output_to_operand_aliasing={{}: (3, {})} | custom-call | flops 671088640 | bytes 2097152 | tf_op jit(solution)/shard_map/pallas_call | solution.py:194
  135.4 0.0 copy-start.8
  135.4 0.0 collective-permute-done.5.pair_ref
  135.4 1.7 %shard_map.98 = (f32[1024,256]{1,0:T(8,128)S(1)}, f32[2,1024]{1,0:T(2,128)S(1)}) custom-call(bf16[1024,256]{1,0:T(8,128)(2,1)S(1)} %get-tuple-element.11.query_ref, s32[1024,128]{1,0:T(8,128)S(1)} %get-tuple-element.12.end_ref, bf16[2,384,256]{2,1,0:T(8,128)(2,1)S(1)} %collective-permute-done.5.pair_ref, ...), custom_call_target="tpu_custom_call", output_to_operand_aliasing={{0}: (3, {})} | custom-call | flops 402653184 | bytes 2097152 | tf_op jit(solution)/shard_map/pallas_call | solution.py:194
  137.1 5.9 %psum.7 = f32[2,1024]{1,0:T(2,128)S(1)} all-reduce(f32[2,1024]{1,0:T(2,128)S(1)} %get-tuple-element.15), channel_id=1, replica_groups=mesh['seq'=128,'tp'=4] {'tp'}, use_global_device_ids=true, to_apply=%region_0.0 | all-reduce | flops 2048 | bytes 16384 | tf_op jit(solution)/shard_map/psum | solution.py:246
  143.0 0.0 copy-done.8
  143.0 1.1 multiply_convert_fusion
  (4 shorter events, 0.1 us)
Async XLA Ops:
  0.0 116.6 %copy-start.2 = (bf16[1024,512]{1,0:T(8,128)(2,1)S(1)}, bf16[1024,512]{1,0:T(8,128)(2,1)}, u32[]{:S(2)}) copy-start(bf16[1024,512]{1,0:T(8,128)(2,1)} %a_ref.1) | copy-start | bytes 3145732
  0.0 83.5 %copy-start.5 = (s32[1024]{0:T(1024)S(1)}, s32[1024]{0:T(1024)}, u32[]{:S(2)}) copy-start(s32[1024]{0:T(1024)} %param.17) | copy-start | bytes 12292
  0.0 83.5 %copy-start.6 = (s32[16]{0:T(128)S(1)}, s32[16]{0:T(128)}, u32[]{:S(2)}) copy-start(s32[16]{0:T(128)} %offset_ref.1) | copy-start | bytes 196
  0.0 83.5 %copy-start.7 = (s32[16]{0:T(128)S(1)}, s32[16]{0:T(128)}, u32[]{:S(2)}) copy-start(s32[16]{0:T(128)} %length_ref.1) | copy-start | bytes 196
  0.0 116.6 %copy-start = (bf16[2048,256]{1,0:T(8,128)(2,1)S(1)}, bf16[2048,256]{1,0:T(8,128)(2,1)}, u32[]{:S(2)}) copy-start(bf16[2048,256]{1,0:T(8,128)(2,1)} %wqb.3) | copy-start | bytes 3145732
  0.0 116.6 %copy-start.1 = (bf16[2048,256]{1,0:T(8,128)(2,1)S(1)}, bf16[2048,256]{1,0:T(8,128)(2,1)}, u32[]{:S(2)}) copy-start(bf16[2048,256]{1,0:T(8,128)(2,1)} %wgb.3) | copy-start | bytes 3145732
  0.0 42.9 %collective-permute-start = (bf16[1024,512]{1,0:T(8,128)(2,1)}, bf16[1024,512]{1,0:T(8,128)(2,1)}, u32[]{:S(2)}, u32[]{:S(2)}) collective-permute-start(bf16[1024,512]{1,0:T(8,128)(2,1)} %a_ref.1), channel_id=1, source_target_pairs={{0,2},{2,0},{1,3},{3,1},{4,6},{6,4},{5,7},{7,5},{8,10},{10,8},{9,1... | collective-permute-start | bytes 3145736 | tf_op jit(solution)/shard_map/ppermute | solution.py:225
  4.6 112.0 %collective-permute-start.2 = (bf16[1024,512]{1,0:T(8,128)(2,1)}, bf16[1024,512]{1,0:T(8,128)(2,1)}, u32[]{:S(2)}, u32[]{:S(2)}) collective-permute-start(bf16[1024,512]{1,0:T(8,128)(2,1)} %a_ref.1), channel_id=1, source_target_pairs={{0,1},{1,0},{2,3},{3,2},{4,5},{5,4},{6,7},{7,6},{8,9},{9,8},{10,11... | collective-permute-start | bytes 3145736 | tf_op jit(solution)/shard_map/ppermute | solution.py:228
  8.6 70.0 %collective-permute-start.6 = (bf16[2,640,256]{2,1,0:T(8,128)(2,1)}, bf16[2,640,256]{2,1,0:T(8,128)(2,1)}, u32[]{:S(2)}, u32[]{:S(2)}) collective-permute-start(bf16[2,640,256]{2,1,0:T(8,128)(2,1)} %pad_maximum_fusion), channel_id=1, source_target_pairs={{0,508},{4,0},{8,4},{12,8},{16,12},{20,16},{24,20},{28,24},{32,28}... | collective-permute-start | bytes 1966088 | tf_op jit(solution)/shard_map/ppermute | solution.py:226
  42.9 77.6 %collective-permute-start.1 = (bf16[1024,512]{1,0:T(8,128)(2,1)}, bf16[1024,512]{1,0:T(8,128)(2,1)}, u32[]{:S(2)}, u32[]{:S(2)}) collective-permute-start(bf16[1024,512]{1,0:T(8,128)(2,1)} %collective-permute-done.a_ref), channel_id=1, source_target_pairs={{0,1},{1,0},{2,3},{3,2},{4,5},{5,4},{6,7},{7,6},{8,9},{9,8},{10,11... | collective-permute-start | bytes 3145736 | tf_op jit(solution)/shard_map/ppermute | solution.py:229
  45.9 30.7 %collective-permute-start.3 = (bf16[2,384,256]{2,1,0:T(8,128)(2,1)S(1)}, bf16[2,384,256]{2,1,0:T(8,128)(2,1)}, u32[]{:S(2)}, u32[]{:S(2)}) collective-permute-start(bf16[2,384,256]{2,1,0:T(8,128)(2,1)S(1)} %pad_maximum_fusion.1), channel_id=1, source_target_pairs={{0,4},{4,8},{8,12},{12,0},{16,20},{20,24},{24,28},{28,16},{32,36},... | collective-permute-start | bytes 1179656 | tf_op jit(solution)/shard_map/ppermute | solution.py:227
  76.7 14.7 %collective-permute-start.4 = (bf16[2,384,256]{2,1,0:T(8,128)(2,1)}, bf16[2,384,256]{2,1,0:T(8,128)(2,1)S(1)}, u32[]{:S(2)}, u32[]{:S(2)}) collective-permute-start(bf16[2,384,256]{2,1,0:T(8,128)(2,1)} %collective-permute-done.3), channel_id=1, source_target_pairs={{0,4},{4,504},{8,508},{12,0},{16,20},{20,8},{24,12},{28,16},{32,36... | collective-permute-start | bytes 1179656 | tf_op jit(solution)/shard_map/ppermute | solution.py:230
  78.6 53.8 %collective-permute-start.7 = (bf16[2,640,256]{2,1,0:T(8,128)(2,1)}, bf16[2,640,256]{2,1,0:T(8,128)(2,1)}, u32[]{:S(2)}, u32[]{:S(2)}) collective-permute-start(bf16[2,640,256]{2,1,0:T(8,128)(2,1)} %collective-permute-done.6.pair_ref), channel_id=1, source_target_pairs={{0,508},{4,0},{8,4},{12,8},{16,12},{20,16},{24,20},{28,24},{32,28}... | collective-permute-start | bytes 1966088 | tf_op jit(solution)/shard_map/ppermute | solution.py:231
  91.3 44.1 %collective-permute-start.5 = (bf16[2,384,256]{2,1,0:T(8,128)(2,1)S(1)}, bf16[2,384,256]{2,1,0:T(8,128)(2,1)S(1)}, u32[]{:S(2)}, u32[]{:S(2)}) collective-permute-start(bf16[2,384,256]{2,1,0:T(8,128)(2,1)S(1)} %collective-permute-done.4.pair_ref), channel_id=1, source_target_pairs={{0,4},{4,8},{8,12},{12,16},{16,20},{20,24},{24,28},{28,32},{32,36}... | collective-permute-start | bytes 1179656 | tf_op jit(solution)/shard_map/ppermute | solution.py:232
  120.5 4.1 %copy-start.3 = (bf16[1024,256]{1,0:T(8,128)(2,1)S(1)}, bf16[1024,256]{1,0:T(8,128)(2,1)}, u32[]{:S(2)}) copy-start(bf16[1024,256]{1,0:T(8,128)(2,1)} %value_ref.1) | copy-start | bytes 1572868
  120.5 4.1 %copy-start.4 = (bf16[1024,256]{1,0:T(8,128)(2,1)S(1)}, bf16[1024,256]{1,0:T(8,128)(2,1)}, u32[]{:S(2)}) copy-start(bf16[1024,256]{1,0:T(8,128)(2,1)} %key_ref.1) | copy-start | bytes 1572868
  135.4 7.6 %copy-start.8 = (f32[256]{0:T(256)S(1)}, f32[256]{0:T(256)}, u32[]{:S(2)}) copy-start(f32[256]{0:T(256)} %param.12) | copy-start | bytes 3076

commit v2 on v1

--- a/solution.py
+++ b/solution.py
@@ -37,6 +37,27 @@
             pairs.append((i, target))
         up.append(pairs)
     return down, up
+
+
+def pack_kernel(key_ref, value_ref, a_ref, b_ref):
+    cut = a_ref.shape[1]
+    for place, ref in enumerate((key_ref, value_ref)):
+        a_ref[place] = ref[:cut]
+        b_ref[place] = ref[cut:]
+
+
+def pack(keys, values, cut):
+    rows, width = keys.shape
+    return pl.pallas_call(
+        pack_kernel,
+        out_shape=(
+            jax.ShapeDtypeStruct((2, cut, width), keys.dtype),
+            jax.ShapeDtypeStruct((2, rows - cut, width), keys.dtype),
+        ),
+        in_specs=[VMEM] * 2,
+        out_specs=(VMEM, VMEM),
+        compiler_params=PARAMS,
+    )(keys, values)
 
 
 def windows_kernel(seq_ref, offset_ref, length_ref, user_ref, start_ref, end_ref):
@@ -220,12 +241,12 @@
     other_chip = [(0, 2), (2, 0), (1, 3), (3, 1)]
     other_core = [(0, 1), (1, 0), (2, 3), (3, 2)]
 
-    pair_a = jnp.stack([hist_keys[:cut], hist_values[:cut]])
-    pair_b = jnp.stack([hist_keys[cut:], hist_values[cut:]])
+    pair_a, pair_b = pack(hist_keys, hist_values, cut)
     far = lax.ppermute(targets, "tp", other_chip)
     next_a = lax.ppermute(pair_a, "seq", down)
     up_b = lax.ppermute(pair_b, "seq", up[0])
     near = lax.ppermute(targets, "tp", other_core)
+    far, up_b = lax.optimization_barrier((far, up_b))
     far_near = lax.ppermute(far, "tp", other_core)
     over_b = lax.ppermute(up_b, "seq", up[1])
     over_a = lax.ppermute(next_a, "seq", down)

time: 145 us -> 117 us (0.81)
  the two profiles are of different devices: /device:TPU:186 before, /device:TPU:1 now
where the time goes in v2:
time: 117 us; the launch traced here: 116 us
  starting transfers between devices  42.3 us (36%)
  waiting for transfers between devices  36.4 us (31%)
  Pallas kernels  19.1 us (16%)
  blocking collectives  8.93 us (8%)
  local copies, waits for them, and re-layouts  7.78 us (7%)
  other arithmetic  1.38 us (1%)
    ppermute x1, waiting for transfers between devices, body(): up_b = lax.ppermute(pair_b, 'seq', up[0])  24.9 us
    ppermute x1, starting transfers between devices, body(): next_a = lax.ppermute(pair_a, 'seq', down)  10.7 us
    pallas_call x4, Pallas kernels, attend_next(): pl.pallas_call(functools.partial(next_kernel, place=place), out_shape=out...  8.98 us
    psum x1, blocking collectives, body(): sums = lax.psum(stats, 'tp') / HQ  8.93 us
    unnamed x26, local copies, waits for them, and re-layouts  7.77 us
    ppermute x1, starting transfers between devices, body(): over_a = lax.ppermute(next_a, 'seq', down)  7.24 us
    ppermute x1, waiting for transfers between devices, body(): over_b = lax.ppermute(up_b, 'seq', up[1])  6.5 us
    ppermute x1, starting transfers between devices, body(): far_near = lax.ppermute(far, 'tp', other_core)  6.06 us
  transfers between devices with their start and end apart: 8, of which 4 were waited for; matrix products, arithmetic and copies ran while one was open for 0% of the time, Pallas kernels for 15%

profile of v2, /device:TPU:1, one launch (start us, length us, event | category | flops | bytes accessed | tf_op | source)
XLA Modules:
  0.0 116.2 jit_solution(8469800031597167198)
XLA Ops:
  0.0 4.8 %collective-permute-start = (bf16[1024,512]{1,0:T(8,128)(2,1)}, bf16[1024,512]{1,0:T(8,128)(2,1)S(1)}, u32[]{:S(2)}, u32[]{:S(2)}) collective-permute-start(bf16[1024,512]{1,0:T(8,128)(2,1)} %a_ref.1), channel_id=1, source_target_pairs={{0,2},{2,0},{1,3},{3,1},{4,6},{6,4},{5,7},{7,5},{8,10},{10,8},{9,1... | collective-permute-start | bytes 3145736 | tf_op jit(solution)/shard_map/ppermute | solution.py:245
  4.8 0.0 copy-start.5
  4.8 1.0 copy-done.5
  5.9 0.0 copy-start.7
  5.9 1.0 copy-done.7
  6.9 0.9 shard_map.91
  7.8 5.8 %collective-permute-start.1 = (bf16[2,384,256]{2,1,0:T(8,128)(2,1)S(1)}, bf16[2,384,256]{2,1,0:T(8,128)(2,1)}, u32[]{:S(2)}, u32[]{:S(2)}) collective-permute-start(bf16[2,384,256]{2,1,0:T(8,128)(2,1)S(1)} %get-tuple-element.15), channel_id=1, source_target_pairs={{0,4},{4,8},{8,12},{12,0},{16,20},{20,24},{24,28},{28,16},{32,36},... | collective-permute-start | bytes 1179656 | tf_op jit(solution)/shard_map/ppermute | solution.py:247
  13.6 3.1 %collective-permute-start.3 = (bf16[1024,512]{1,0:T(8,128)(2,1)}, bf16[1024,512]{1,0:T(8,128)(2,1)S(1)}, u32[]{:S(2)}, u32[]{:S(2)}) collective-permute-start(bf16[1024,512]{1,0:T(8,128)(2,1)} %a_ref.1), channel_id=1, source_target_pairs={{0,1},{1,0},{2,3},{3,2},{4,5},{5,4},{6,7},{7,6},{8,9},{9,8},{10,11... | collective-permute-start | bytes 3145736 | tf_op jit(solution)/shard_map/ppermute | solution.py:248
  16.8 10.7 %collective-permute-start.6 = (bf16[2,640,256]{2,1,0:T(8,128)(2,1)}, bf16[2,640,256]{2,1,0:T(8,128)(2,1)}, u32[]{:S(2)}, u32[]{:S(2)}) collective-permute-start(bf16[2,640,256]{2,1,0:T(8,128)(2,1)} %get-tuple-element.20), channel_id=1, source_target_pairs={{0,508},{4,0},{8,4},{12,8},{16,12},{20,16},{24,20},{28,24},{32,28}... | collective-permute-start | bytes 1966088 | tf_op jit(solution)/shard_map/ppermute | solution.py:246
  27.5 24.9 %collective-permute-done.1 = bf16[2,384,256]{2,1,0:T(8,128)(2,1)} collective-permute-done((bf16[2,384,256]{2,1,0:T(8,128)(2,1)S(1)}, bf16[2,384,256]{2,1,0:T(8,128)(2,1)}, u32[]{:S(2)}, u32[]{:S(2)}) %collective-permute-start.1) | collective-permute-done | bytes 393248 | tf_op jit(solution)/shard_map/ppermute | solution.py:247
  52.4 0.0 collective-permute-done.a_ref
  52.4 6.1 %collective-permute-start.2 = (bf16[1024,512]{1,0:T(8,128)(2,1)S(1)}, bf16[1024,512]{1,0:T(8,128)(2,1)S(1)}, u32[]{:S(2)}, u32[]{:S(2)}) collective-permute-start(bf16[1024,512]{1,0:T(8,128)(2,1)S(1)} %collective-permute-done.a_ref), channel_id=1, source_target_pairs={{0,1},{1,0},{2,3},{3,2},{4,5},{5,4},{6,7},{7,6},{8,9},{9,8},{10,11... | collective-permute-start | bytes 3145736 | tf_op jit(solution)/shard_map/ppermute | solution.py:250
  58.5 1.9 %collective-permute-start.4 = (bf16[2,384,256]{2,1,0:T(8,128)(2,1)}, bf16[2,384,256]{2,1,0:T(8,128)(2,1)S(1)}, u32[]{:S(2)}, u32[]{:S(2)}) collective-permute-start(bf16[2,384,256]{2,1,0:T(8,128)(2,1)} %collective-permute-done.1), channel_id=1, source_target_pairs={{0,4},{4,504},{8,508},{12,0},{16,20},{20,8},{24,12},{28,16},{32,36... | collective-permute-start | bytes 1179656 | tf_op jit(solution)/shard_map/ppermute | solution.py:251
  60.4 0.7 collective-permute-done.6.pair_ref
  61.1 7.2 %collective-permute-start.7 = (bf16[2,640,256]{2,1,0:T(8,128)(2,1)}, bf16[2,640,256]{2,1,0:T(8,128)(2,1)}, u32[]{:S(2)}, u32[]{:S(2)}) collective-permute-start(bf16[2,640,256]{2,1,0:T(8,128)(2,1)} %collective-permute-done.6.pair_ref), channel_id=1, source_target_pairs={{0,508},{4,0},{8,4},{12,8},{16,12},{20,16},{24,20},{28,24},{32,28}... | collective-permute-start | bytes 1966088 | tf_op jit(solution)/shard_map/ppermute | solution.py:252
  68.4 0.1 pad_add_fusion.2.seq_ref
  68.4 0.0 copy-start.9
  68.4 0.7 copy-done.9
  69.1 0.0 copy-start.10
  69.1 0.7 copy-done.10
  69.8 0.0 copy-start.11
  69.8 0.7 copy-done.11
  70.4 0.9 shard_map.94
  71.4 0.1 pad_add_fusion.1.order_ref
  71.4 0.1 pad_add_fusion.order_ref
  71.5 6.5 %collective-permute-done.4.pair_ref = bf16[2,384,256]{2,1,0:T(8,128)(2,1)S(1)} collective-permute-done((bf16[2,384,256]{2,1,0:T(8,128)(2,1)}, bf16[2,384,256]{2,1,0:T(8,128)(2,1)S(1)}, u32[]{:S(2)}, u32[]{:S(2)}) %collective-permute-start.4) | collective-permute-done | bytes 393248 | tf_op jit(solution)/shard_map/ppermute | solution.py:251
  78.0 2.7 %collective-permute-start.5 = (bf16[2,384,256]{2,1,0:T(8,128)(2,1)S(1)}, bf16[2,384,256]{2,1,0:T(8,128)(2,1)S(1)}, u32[]{:S(2)}, u32[]{:S(2)}) collective-permute-start(bf16[2,384,256]{2,1,0:T(8,128)(2,1)S(1)} %collective-permute-done.4.pair_ref), channel_id=1, source_target_pairs={{0,4},{4,8},{8,12},{12,16},{16,20},{20,24},{24,28},{28,32},{32,36}... | collective-permute-start | bytes 1179656 | tf_op jit(solution)/shard_map/ppermute | solution.py:253
  80.7 0.0 collective-permute-done.3.b_ref
  80.7 0.0 copy-start
  80.7 1.2 %copy-done = bf16[2048,256]{1,0:T(8,128)(2,1)S(1)} copy-done((bf16[2048,256]{1,0:T(8,128)(2,1)S(1)}, bf16[2048,256]{1,0:T(8,128)(2,1)}, u32[]{:S(2)}) %copy-start) | copy-done | bytes 1048600
  81.9 0.0 copy-start.2
  81.9 1.2 %copy-done.2 = bf16[2048,256]{1,0:T(8,128)(2,1)S(1)} copy-done((bf16[2048,256]{1,0:T(8,128)(2,1)S(1)}, bf16[2048,256]{1,0:T(8,128)(2,1)}, u32[]{:S(2)}) %copy-start.2) | copy-done | bytes 1048600
  83.2 0.0 copy-start.4
  83.2 1.2 %copy-done.4 = bf16[1024,512]{1,0:T(8,128)(2,1)S(1)} copy-done((bf16[1024,512]{1,0:T(8,128)(2,1)S(1)}, bf16[1024,512]{1,0:T(8,128)(2,1)}, u32[]{:S(2)}) %copy-start.4) | copy-done | bytes 1048600
  84.4 0.0 copy-start.1
  84.4 0.0 copy-start.3
  84.4 2.3 %shard_map.92.refs_0_ = f32[1024,512]{1,0:T(8,128)S(1)} custom-call(s32[2]{0:T(128)S(1)} %pad_add_fusion.1.order_ref, bf16[1024,512]{1,0:T(8,128)(2,1)S(1)} %copy-done.4, bf16[1024,512]{1,0:T(8,128)(2,1)S(1)} %collective-permute-done.3.b_ref, bf16[2048,256]{1,0:T(8,128)(2,1)S(1)} %copy-done, bf16[2048,256]{1,0:T(8,128)(2,1)S(1)} %copy-done, ...), custom_call_target="tpu_custom_call" | custom-call | flops 1073741824 | bytes 4194304 | tf_op jit(solution)/shard_map/pallas_call | solution.py:130
  86.7 0.0 copy-start.6
  86.7 0.0 copy-start.8
  86.8 0.0 collective-permute-done.2.b_ref
  86.8 0.0 copy-done.1
  86.8 0.0 copy-done.3
  86.8 2.4 %shard_map.93 = (bf16[1024,256]{1,0:T(8,128)(2,1)S(1)}, f32[1024,256]{1,0:T(8,128)S(1)}) custom-call(s32[2]{0:T(128)S(1)} %pad_add_fusion.order_ref, bf16[1024,512]{1,0:T(8,128)(2,1)S(1)} %collective-permute-done.a_ref, bf16[1024,512]{1,0:T(8,128)(2,1)S(1)} %collective-permute-done.2.b_ref, bf16[2048,256]{1,0:T(8,128)(2,1)S(1)} %copy-done.1, ...), custom_call_target="tpu_custom_call" | custom-call | flops 1073741824 | bytes 4194304 | tf_op jit(solution)/shard_map/pallas_call | solution.py:130
  89.2 0.0 copy-done.6
  89.2 0.0 copy-done.8
  89.2 3.5 %shard_map.95.total_ref = f32[1024,256]{1,0:T(8,128)S(1)} custom-call(bf16[1024,256]{1,0:T(8,128)(2,1)S(1)} %get-tuple-element.17.query_ref, s32[1024,128]{1,0:T(8,128)S(1)} %get-tuple-element.21.start_ref, s32[1024,128]{1,0:T(8,128)S(1)} %get-tuple-element.18.end_ref, bf16[1024,256]{1,0:T(8,128)(2,1)S(1)} %copy-done.6, bf16[1024,256]{1,0:T(8,128)(2,1)S(1)} %copy-done.8), custom_call_target="tpu_custom_call" | custom-call | flops 1073741824 | bytes 2097152 | tf_op jit(solution)/shard_map/pallas_call | solution.py:201
  92.8 3.0 %shard_map.96.total_ref = f32[1024,256]{1,0:T(8,128)S(1)} custom-call(bf16[1024,256]{1,0:T(8,128)(2,1)S(1)} %get-tuple-element.17.query_ref, s32[1024,128]{1,0:T(8,128)S(1)} %get-tuple-element.18.end_ref, bf16[2,640,256]{2,1,0:T(8,128)(2,1)} %collective-permute-done.6.pair_ref, f32[1024,256]{1,0:T(8,128)S(1)} %shard_map.95.total_ref), custom_call_target="tpu_custom_call", output_to_operand_aliasing={{}: (3, {})} | custom-call | flops 671088640 | bytes 2097152 | tf_op jit(solution)/shard_map/pallas_call | solution.py:215
  95.7 1.4 %shard_map.97.total_ref = f32[1024,256]{1,0:T(8,128)S(1)} custom-call(bf16[1024,256]{1,0:T(8,128)(2,1)S(1)} %get-tuple-element.17.query_ref, s32[1024,128]{1,0:T(8,128)S(1)} %get-tuple-element.18.end_ref, bf16[2,384,256]{2,1,0:T(8,128)(2,1)S(1)} %collective-permute-done.4.pair_ref, f32[1024,256]{1,0:T(8,128)S(1)} %shard_map.96.total_ref), custom_call_target="tpu_custom_call", output_to_operand_aliasing={{}: (3, {})} | custom-call | flops 402653184 | bytes 2097152 | tf_op jit(solution)/shard_map/pallas_call | solution.py:215
  97.1 0.0 collective-permute-done.7.pair_ref
  97.1 3.0 %shard_map.98.total_ref = f32[1024,256]{1,0:T(8,128)S(1)} custom-call(bf16[1024,256]{1,0:T(8,128)(2,1)S(1)} %get-tuple-element.17.query_ref, s32[1024,128]{1,0:T(8,128)S(1)} %get-tuple-element.18.end_ref, bf16[2,640,256]{2,1,0:T(8,128)(2,1)} %collective-permute-done.7.pair_ref, f32[1024,256]{1,0:T(8,128)S(1)} %shard_map.97.total_ref), custom_call_target="tpu_custom_call", output_to_operand_aliasing={{}: (3, {})} | custom-call | flops 671088640 | bytes 2097152 | tf_op jit(solution)/shard_map/pallas_call | solution.py:215
  100.1 0.0 copy-start.12
  100.1 4.2 %collective-permute-done.5.pair_ref = bf16[2,384,256]{2,1,0:T(8,128)(2,1)S(1)} collective-permute-done((bf16[2,384,256]{2,1,0:T(8,128)(2,1)S(1)}, bf16[2,384,256]{2,1,0:T(8,128)(2,1)S(1)}, u32[]{:S(2)}, u32[]{:S(2)}) %collective-permute-start.5) | collective-permute-done | bytes 393248 | tf_op jit(solution)/shard_map/ppermute | solution.py:253
  104.3 1.7 %shard_map.99 = (f32[1024,256]{1,0:T(8,128)S(1)}, f32[2,1024]{1,0:T(2,128)S(1)}) custom-call(bf16[1024,256]{1,0:T(8,128)(2,1)S(1)} %get-tuple-element.17.query_ref, s32[1024,128]{1,0:T(8,128)S(1)} %get-tuple-element.18.end_ref, bf16[2,384,256]{2,1,0:T(8,128)(2,1)S(1)} %collective-permute-done.5.pair_ref, ...), custom_call_target="tpu_custom_call", output_to_operand_aliasing={{0}: (3, {})} | custom-call | flops 402653184 | bytes 2097152 | tf_op jit(solution)/shard_map/pallas_call | solution.py:215
  106.0 8.9 %psum.7 = f32[2,1024]{1,0:T(2,128)S(1)} all-reduce(f32[2,1024]{1,0:T(2,128)S(1)} %get-tuple-element.23), channel_id=1, replica_groups=mesh['seq'=128,'tp'=4] {'tp'}, use_global_device_ids=true, to_apply=%region_0.0 | all-reduce | flops 2048 | bytes 16384 | tf_op jit(solution)/shard_map/psum | solution.py:267
  115.0 0.0 copy-done.12
  115.0 1.1 multiply_convert_fusion
  (3 shorter events, 0.0 us)
Async XLA Ops:
  0.0 52.4 %collective-permute-start = (bf16[1024,512]{1,0:T(8,128)(2,1)}, bf16[1024,512]{1,0:T(8,128)(2,1)S(1)}, u32[]{:S(2)}, u32[]{:S(2)}) collective-permute-start(bf16[1024,512]{1,0:T(8,128)(2,1)} %a_ref.1), channel_id=1, source_target_pairs={{0,2},{2,0},{1,3},{3,1},{4,6},{6,4},{5,7},{7,5},{8,10},{10,8},{9,1... | collective-permute-start | bytes 3145736 | tf_op jit(solution)/shard_map/ppermute | solution.py:245
  4.8 1.0 copy-start.5
  5.9 1.0 copy-start.7
  7.8 44.5 %collective-permute-start.1 = (bf16[2,384,256]{2,1,0:T(8,128)(2,1)S(1)}, bf16[2,384,256]{2,1,0:T(8,128)(2,1)}, u32[]{:S(2)}, u32[]{:S(2)}) collective-permute-start(bf16[2,384,256]{2,1,0:T(8,128)(2,1)S(1)} %get-tuple-element.15), channel_id=1, source_target_pairs={{0,4},{4,8},{8,12},{12,0},{16,20},{20,24},{24,28},{28,16},{32,36},... | collective-permute-start | bytes 1179656 | tf_op jit(solution)/shard_map/ppermute | solution.py:247
  13.6 67.0 %collective-permute-start.3 = (bf16[1024,512]{1,0:T(8,128)(2,1)}, bf16[1024,512]{1,0:T(8,128)(2,1)S(1)}, u32[]{:S(2)}, u32[]{:S(2)}) collective-permute-start(bf16[1024,512]{1,0:T(8,128)(2,1)} %a_ref.1), channel_id=1, source_target_pairs={{0,1},{1,0},{2,3},{3,2},{4,5},{5,4},{6,7},{7,6},{8,9},{9,8},{10,11... | collective-permute-start | bytes 3145736 | tf_op jit(solution)/shard_map/ppermute | solution.py:248
  16.8 44.3 %collective-permute-start.6 = (bf16[2,640,256]{2,1,0:T(8,128)(2,1)}, bf16[2,640,256]{2,1,0:T(8,128)(2,1)}, u32[]{:S(2)}, u32[]{:S(2)}) collective-permute-start(bf16[2,640,256]{2,1,0:T(8,128)(2,1)} %get-tuple-element.20), channel_id=1, source_target_pairs={{0,508},{4,0},{8,4},{12,8},{16,12},{20,16},{24,20},{28,24},{32,28}... | collective-permute-start | bytes 1966088 | tf_op jit(solution)/shard_map/ppermute | solution.py:246
  52.4 34.4 %collective-permute-start.2 = (bf16[1024,512]{1,0:T(8,128)(2,1)S(1)}, bf16[1024,512]{1,0:T(8,128)(2,1)S(1)}, u32[]{:S(2)}, u32[]{:S(2)}) collective-permute-start(bf16[1024,512]{1,0:T(8,128)(2,1)S(1)} %collective-permute-done.a_ref), channel_id=1, source_target_pairs={{0,1},{1,0},{2,3},{3,2},{4,5},{5,4},{6,7},{7,6},{8,9},{9,8},{10,11... | collective-permute-start | bytes 3145736 | tf_op jit(solution)/shard_map/ppermute | solution.py:250
  58.5 19.5 %collective-permute-start.4 = (bf16[2,384,256]{2,1,0:T(8,128)(2,1)}, bf16[2,384,256]{2,1,0:T(8,128)(2,1)S(1)}, u32[]{:S(2)}, u32[]{:S(2)}) collective-permute-start(bf16[2,384,256]{2,1,0:T(8,128)(2,1)} %collective-permute-done.1), channel_id=1, source_target_pairs={{0,4},{4,504},{8,508},{12,0},{16,20},{20,8},{24,12},{28,16},{32,36... | collective-permute-start | bytes 1179656 | tf_op jit(solution)/shard_map/ppermute | solution.py:251
  61.1 36.0 %collective-permute-start.7 = (bf16[2,640,256]{2,1,0:T(8,128)(2,1)}, bf16[2,640,256]{2,1,0:T(8,128)(2,1)}, u32[]{:S(2)}, u32[]{:S(2)}) collective-permute-start(bf16[2,640,256]{2,1,0:T(8,128)(2,1)} %collective-permute-done.6.pair_ref), channel_id=1, source_target_pairs={{0,508},{4,0},{8,4},{12,8},{16,12},{20,16},{24,20},{28,24},{32,28}... | collective-permute-start | bytes 1966088 | tf_op jit(solution)/shard_map/ppermute | solution.py:252
  68.4 0.7 copy-start.9
  69.1 0.7 copy-start.10
  69.8 0.7 copy-start.11
  78.0 26.3 %collective-permute-start.5 = (bf16[2,384,256]{2,1,0:T(8,128)(2,1)S(1)}, bf16[2,384,256]{2,1,0:T(8,128)(2,1)S(1)}, u32[]{:S(2)}, u32[]{:S(2)}) collective-permute-start(bf16[2,384,256]{2,1,0:T(8,128)(2,1)S(1)} %collective-permute-done.4.pair_ref), channel_id=1, source_target_pairs={{0,4},{4,8},{8,12},{12,16},{16,20},{20,24},{24,28},{28,32},{32,36}... | collective-permute-start | bytes 1179656 | tf_op jit(solution)/shard_map/ppermute | solution.py:253
  80.7 1.2 %copy-start = (bf16[2048,256]{1,0:T(8,128)(2,1)S(1)}, bf16[2048,256]{1,0:T(8,128)(2,1)}, u32[]{:S(2)}) copy-start(bf16[2048,256]{1,0:T(8,128)(2,1)} %wqb.3) | copy-start | bytes 3145732
  81.9 1.2 %copy-start.2 = (bf16[2048,256]{1,0:T(8,128)(2,1)S(1)}, bf16[2048,256]{1,0:T(8,128)(2,1)}, u32[]{:S(2)}) copy-start(bf16[2048,256]{1,0:T(8,128)(2,1)} %wgb.3) | copy-start | bytes 3145732
  83.2 1.2 %copy-start.4 = (bf16[1024,512]{1,0:T(8,128)(2,1)S(1)}, bf16[1024,512]{1,0:T(8,128)(2,1)}, u32[]{:S(2)}) copy-start(bf16[1024,512]{1,0:T(8,128)(2,1)} %a_ref.1) | copy-start | bytes 3145732
  84.4 2.4 %copy-start.1 = (bf16[2048,256]{1,0:T(8,128)(2,1)S(1)}, bf16[2048,256]{1,0:T(8,128)(2,1)}, u32[]{:S(2)}) copy-start(bf16[2048,256]{1,0:T(8,128)(2,1)} %wqb.3) | copy-start | bytes 3145732
  84.4 2.4 %copy-start.3 = (bf16[2048,256]{1,0:T(8,128)(2,1)S(1)}, bf16[2048,256]{1,0:T(8,128)(2,1)}, u32[]{:S(2)}) copy-start(bf16[2048,256]{1,0:T(8,128)(2,1)} %wgb.3) | copy-start | bytes 3145732
  86.7 2.5 %copy-start.6 = (bf16[1024,256]{1,0:T(8,128)(2,1)S(1)}, bf16[1024,256]{1,0:T(8,128)(2,1)}, u32[]{:S(2)}) copy-start(bf16[1024,256]{1,0:T(8,128)(2,1)} %key_ref.3) | copy-start | bytes 1572868
  86.7 2.5 %copy-start.8 = (bf16[1024,256]{1,0:T(8,128)(2,1)S(1)}, bf16[1024,256]{1,0:T(8,128)(2,1)}, u32[]{:S(2)}) copy-start(bf16[1024,256]{1,0:T(8,128)(2,1)} %value_ref.3) | copy-start | bytes 1572868
  100.1 14.9 %copy-start.12 = (f32[256]{0:T(256)S(1)}, f32[256]{0:T(256)}, u32[]{:S(2)}) copy-start(f32[256]{0:T(256)} %param.12) | copy-start | bytes 3076

commit v3 on v1

v3 whole, which is shorter than its diff:
```python
import functools

import jax
import jax.numpy as jnp
from jax import lax
from jax.experimental import pallas as pl
from jax.experimental.pallas import tpu as pltpu
from jax.sharding import PartitionSpec as P

HDIM = 128
U_DEV = 16
HQ = 1024
Z_HI = 4
LANES = 128
DOWN = (624,)
UP = (400,)
VMEM = pl.BlockSpec(memory_space=pltpu.VMEM)
HBM = pl.BlockSpec(memory_space=pltpu.HBM)
SMEM = pl.BlockSpec(memory_space=pltpu.SMEM)
FULL = pltpu.CompilerParams(vmem_limit_bytes=60 * 2**20)
PARAMS = pltpu.CompilerParams(vmem_limit_bytes=40 * 2**20)


def ring_perms(n_seq):
    down = [(i, (i - 1) % n_seq) for i in range(n_seq)]
    up = []
    for stage in range(3):
        pairs = []
        for i in range(n_seq):
            column, z = divmod(i, Z_HI)
            origin = (z - stage) % Z_HI
            shift = 0
            if stage == 1 and origin == 0:
                shift = -1
            if stage == 1 and origin == 1:
                shift = -1
            if stage == 2 and origin == 1:
                shift = 1
            target = (column + shift) % (n_seq // Z_HI) * Z_HI + (z + 1) % Z_HI
            pairs.append((i, target))
        up.append(pairs)
    return down, up


def pack_kernel(chunks, key_ref, value_ref, *refs):
    outs, sems = refs[:-1], refs[-1]
    copies = []
    for (at, size), out in zip(chunks, outs):
        for place, ref in enumerate((key_ref, value_ref)):
            copies.append(
                pltpu.make_async_copy(ref.at[pl.ds(at, size)], out.at[place], sems.at[len(copies)])
            )
    for copy in copies:
        copy.start()
    for copy in copies:
        copy.wait()


def pack(keys, values, chunks):
    width = keys.shape[1]
    return pl.pallas_call(
        functools.partial(pack_kernel, chunks),
        out_shape=[jax.ShapeDtypeStruct((2, size, width), keys.dtype) for _, size in chunks],
        in_specs=[HBM] * 2,
        out_specs=[VMEM] * len(chunks),
        scratch_shapes=[pltpu.SemaphoreType.DMA((2 * len(chunks),))],
        cost_estimate=pl.CostEstimate(flops=1, bytes_accessed=1, transcendentals=0),
        compiler_params=FULL,
    )(keys, values)


def windows_kernel(seq_ref, offset_ref, length_ref, user_ref, start_ref, end_ref):
    first_user = seq_ref[0] * U_DEV
    first_row = seq_ref[0] * seq_ref[1]
    user = user_ref[...] - first_user
    start = jnp.zeros_like(user)
    end = jnp.zeros_like(user)
    for u in range(U_DEV):
        mine = user == u
        low = offset_ref[u] - first_row
        start = jnp.where(mine, low, start)
        end = jnp.where(mine, low + length_ref[u], end)
    for group in range(user.shape[0]):
        rows = slice(group * LANES, (group + 1) * LANES)
        start_ref[rows, :] = jnp.broadcast_to(start[group : group + 1], (LANES, LANES)).T
        end_ref[rows, :] = jnp.broadcast_to(end[group : group + 1], (LANES, LANES)).T


def windows(seq_info, user_offset, user_length, target_user):
    rows = target_user.shape[0]
    wide = jax.ShapeDtypeStruct((rows, LANES), jnp.int32)
    return pl.pallas_call(
        windows_kernel,
        out_shape=(wide, wide),
        in_specs=[SMEM, SMEM, SMEM, VMEM],
        out_specs=(VMEM, VMEM),
        cost_estimate=pl.CostEstimate(flops=20000000000, bytes_accessed=1, transcendentals=0),
        compiler_params=FULL,
    )(seq_info, user_offset, user_length, target_user.reshape(rows // LANES, LANES))


def project_kernel(order_ref, *refs):
    features, refs = [ref[...] for ref in refs[:4]], refs[4:]
    sums = []
    for weights in (refs[0:4], refs[4:8]):
        dots = [
            jnp.dot(feature, weight[...], preferred_element_type=jnp.float32)
            for feature, weight in zip(features, weights)
        ]
        sums.append(dots[0] + dots[1] + (dots[2] + dots[3]))
    query_ref, gate_ref = refs[8:]
    query_ref[...] = sums[0].astype(jnp.bfloat16)
    gate_ref[...] = jax.nn.silu(sums[1])


def project(order, pieces, w_query, w_gate, flops=1):
    rows, depth = pieces[0].shape
    width = w_query.shape[1]
    tile = 256
    feature = pl.BlockSpec((tile, depth), lambda i, order: (i, 0))
    weight = [pl.BlockSpec((depth, width), lambda i, order, k=k: (order[k], 0)) for k in range(4)]
    half = pl.BlockSpec((tile, width), lambda i, order: (i, 0))
    return pl.pallas_call(
        project_kernel,
        out_shape=(
            jax.ShapeDtypeStruct((rows, width), jnp.bfloat16),
            jax.ShapeDtypeStruct((rows, width), jnp.float32),
        ),
        grid_spec=pltpu.PrefetchScalarGridSpec(
            num_scalar_prefetch=1,
            grid=(rows // tile,),
            in_specs=[feature] * 4 + weight * 2,
            out_specs=(half, half),
        ),
        compiler_params=PARAMS,
        cost_estimate=pl.CostEstimate(flops=flops, bytes_accessed=1, transcendentals=0),
    )(order, *pieces, *[w_query] * 4, *[w_gate] * 4)


def weigh(query, keys, values, start, end, place, total):
    rows = query.shape[0]
    for at in range(0, keys.shape[0], 256):
        size = min(256, keys.shape[0] - at)
        scores = lax.dot_general(
            query, keys[at : at + size], (((1,), (1,)), ((), ())), preferred_element_type=jnp.float32
        )
        columns = []
        for lane in range(0, size, LANES):
            lanes = min(LANES, size - lane)
            half = scores[:, lane : lane + lanes] * (0.5 * HDIM**-0.5)
            weight = half * jnp.tanh(half) + half
            position = lax.broadcasted_iota(jnp.int32, (rows, lanes), 1) + (place + at + lane)
            inside = position < end[:, :lanes]
            if start is not None:
                inside = inside & (position >= start[:, :lanes])
            columns.append(jnp.where(inside, weight, 0.0).astype(jnp.bfloat16))
        total = total + jnp.dot(
            jnp.concatenate(columns, axis=1), values[at : at + size], preferred_element_type=jnp.float32
        )
    return total


def own_kernel(query_ref, start_ref, end_ref, key_ref, value_ref, out_ref):
    for head in range(query_ref.shape[1] // HDIM):
        cols = slice(head * HDIM, (head + 1) * HDIM)
        zero = jnp.zeros((query_ref.shape[0], HDIM), jnp.float32)
        out_ref[:, cols] = weigh(
            query_ref[:, cols], key_ref[:, cols], value_ref[:, cols], start_ref[...], end_ref[...], 0, zero
        )


def next_kernel(query_ref, end_ref, *refs, places):
    pairs, (total_ref, out_ref, *stats) = refs[: len(places)], refs[len(places) :]
    parts = []
    for head in range(query_ref.shape[1] // HDIM):
        cols = slice(head * HDIM, (head + 1) * HDIM)
        part = total_ref[:, cols]
        for place, pair_ref in zip(places, pairs):
            part = weigh(
                query_ref[:, cols], pair_ref[0, :, cols], pair_ref[1, :, cols], None, end_ref[...], place, part
            )
        out_ref[:, cols] = part
        parts.append(part)
    if stats:
        (stats_ref,) = stats
        plain = functools.reduce(jnp.add, parts)
        square = functools.reduce(jnp.add, [part * part for part in parts])
        for group in range(plain.shape[0] // LANES):
            rows = slice(group * LANES, (group + 1) * LANES)
            stats_ref[0:1, rows] = jnp.sum(plain[rows].T, axis=0, keepdims=True)
            stats_ref[1:2, rows] = jnp.sum(square[rows].T, axis=0, keepdims=True)


def attend_cost(rows, history, width):
    return pl.CostEstimate(flops=1, bytes_accessed=1, transcendentals=0)


def attend_own(query, start, end, keys, values, flops=1):
    return pl.pallas_call(
        own_kernel,
        out_shape=jax.ShapeDtypeStruct(query.shape, jnp.float32),
        in_specs=[VMEM] * 5,
        out_specs=VMEM,
        compiler_params=PARAMS,
        cost_estimate=pl.CostEstimate(flops=flops, bytes_accessed=1, transcendentals=0),
    )(query, start, end, keys, values)


def attend_next(query, end, chunks, total, last=False, flops=1):
    pairs, places = zip(*chunks)
    out_shape = [jax.ShapeDtypeStruct(query.shape, jnp.float32)]
    if last:
        out_shape.append(jax.ShapeDtypeStruct((2, query.shape[0]), jnp.float32))
    history = sum(pair.shape[1] for pair in pairs)
    out = pl.pallas_call(
        functools.partial(next_kernel, places=places),
        out_shape=out_shape,
        in_specs=[VMEM] * (3 + len(pairs)),
        out_specs=[VMEM] * len(out_shape),
        input_output_aliases={2 + len(pairs): 0},
        compiler_params=PARAMS,
        cost_estimate=pl.CostEstimate(flops=flops, bytes_accessed=1, transcendentals=0),
    )(query, end, *pairs, total)
    return out if last else out[0]


def after(array, *others):
    return lax.optimization_barrier((array, *others))[0]


def body(
    targets,
    w_query,
    w_gate,
    norm_gain,
    hist_keys,
    hist_values,
    user_offset,
    user_length,
    target_user,
):
    hist_rows = hist_keys.shape[0]
    down, up = ring_perms(lax.axis_size("seq"))
    other_chip = [(0, 2), (2, 0), (1, 3), (3, 1)]
    other_core = [(0, 1), (1, 0), (2, 3), (3, 2)]
    sizes = DOWN + UP
    at = [sum(sizes[:i]) for i in range(len(sizes))]
    chunks = tuple(zip(at, sizes))

    me = lax.axis_index("tp").astype(jnp.int32)
    seq_info = jnp.stack([lax.axis_index("seq").astype(jnp.int32), jnp.int32(hist_rows)])
    start, end = windows(seq_info, user_offset, user_length, target_user)
    a, b = pack(hist_keys, hist_values, chunks)
    far = lax.ppermute(targets, "tp", other_chip)
    b1 = lax.ppermute(b, "seq", up[0])
    a1 = lax.ppermute(a, "seq", down)
    far = after(far, b1)
    near = lax.ppermute(after(targets, far), "tp", other_core)
    far_near = lax.ppermute(far, "tp", other_core)
    b2 = lax.ppermute(b1, "seq", up[1])
    a2 = lax.ppermute(a1, "seq", down)
    order = jnp.stack([me, me ^ 1, me ^ 2, me ^ 3])
    query, gate = project(order, (targets, near, far, far_near), w_query, w_gate, flops=500000000)
    total = attend_own(query, start, end, hist_keys, hist_values, flops=1000000000)
    b2 = after(b2, query)
    b3 = lax.ppermute(b2, "seq", up[2])
    one, two = hist_rows, 2 * hist_rows
    total = attend_next(query, end, [(a1, one + at[0])], total, flops=500000000)
    total = attend_next(query, end, [(b2, two + at[1])], total, flops=4000000000)
    total = attend_next(query, end, [(a2, two + at[0])], total, flops=4000000000)
    attended, stats = attend_next(query, end, [(b3, one + at[1])], total, flops=4000000000, last=True)

    sums = lax.psum(stats, "tp") / HQ
    mean = sums[0]
    var = sums[1] - mean * mean
    normed = (attended - mean[:, None]) / jnp.sqrt(var[:, None] + 1e-05)
    return (normed * norm_gain[None, :] * gate).astype(jnp.bfloat16)


def solution(mesh):
    return jax.shard_map(
        body,
        mesh=mesh,
        in_specs=(
            P("seq", "tp"),
            P(None, "tp"),
            P(None, "tp"),
            P("tp"),
            P("seq", "tp"),
            P("seq", "tp"),
            P("seq"),
            P("seq"),
            P("seq"),
        ),
        out_specs=P("seq", "tp"),
        check_vma=False,
    )
```

time: 145 us -> 118 us (0.81)
  the two profiles are of different devices: /device:TPU:186 before, /device:TPU:1 now
where the time goes in v3:
time: 118 us; the launch traced here: 117 us
  waiting for transfers between devices  43.7 us (37%)
  starting transfers between devices  41.8 us (35%)
  Pallas kernels  21.2 us (18%)
  blocking collectives  6.75 us (6%)
  other arithmetic  1.82 us (2%)
  local copies, waits for them, and re-layouts  1.69 us (1%)
    ppermute x1, waiting for transfers between devices, body(): b1 = lax.ppermute(b, 'seq', up[0])  37.4 us
    ppermute x1, starting transfers between devices, body(): a1 = lax.ppermute(a, 'seq', down)  11 us
    ppermute x1, starting transfers between devices, body(): a2 = lax.ppermute(a1, 'seq', down)  10.8 us
    pallas_call x4, Pallas kernels, attend_next(): pl.pallas_call(functools.partial(next_kernel, places=places), out_shape=o...  8.25 us
    psum x1, blocking collectives, body(): sums = lax.psum(stats, 'tp') / HQ  6.75 us
    ppermute x1, waiting for transfers between devices, body(): b3 = lax.ppermute(b2, 'seq', up[2])  6.26 us
    ppermute x1, starting transfers between devices, body(): b1 = lax.ppermute(b, 'seq', up[0])  5.81 us
    pallas_call x1, Pallas kernels, project(): pl.pallas_call(project_kernel, out_shape=(jax.ShapeDtypeStruct((rows, wid...  5.07 us
  transfers between devices with their start and end apart: 8, of which 2 were waited for; matrix products, arithmetic and copies ran while one was open for 1% of the time, Pallas kernels for 17%

profile of v3, /device:TPU:1, one launch (start us, length us, event | category | flops | bytes accessed | tf_op | source)
XLA Modules:
  0.0 117.3 jit_solution(4919454242071282007)
XLA Ops:
  0.0 0.0 copy-start.2
  0.0 5.0 %collective-permute-start = (bf16[1024,512]{1,0:T(8,128)(2,1)}, bf16[1024,512]{1,0:T(8,128)(2,1)}, u32[]{:S(2)}, u32[]{:S(2)}) collective-permute-start(bf16[1024,512]{1,0:T(8,128)(2,1)} %refs_0_.1), channel_id=1, source_target_pairs={{0,2},{2,0},{1,3},{3,1},{4,6},{6,4},{5,7},{7,5},{8,10},{10,8},{9,1... | collective-permute-start | bytes 3145736 | tf_op jit(solution)/shard_map/ppermute | solution.py:254
  5.0 2.2 %shard_map.91 = (bf16[2,624,256]{2,1,0:T(8,128)(2,1)}, bf16[2,400,256]{2,1,0:T(8,128)(2,1)}) custom-call(bf16[1024,256]{1,0:T(8,128)(2,1)} %key_ref.3, bf16[1024,256]{1,0:T(8,128)(2,1)} %value_ref.3), custom_call_target="tpu_custom_call" | custom-call | flops 1 | bytes 1 | tf_op jit(solution)/shard_map/pallas_call | solution.py:61
  7.2 5.8 %collective-permute-start.1 = (bf16[2,400,256]{2,1,0:T(8,128)(2,1)}, bf16[2,400,256]{2,1,0:T(8,128)(2,1)}, u32[]{:S(2)}, u32[]{:S(2)}) collective-permute-start(bf16[2,400,256]{2,1,0:T(8,128)(2,1)} %get-tuple-element.16), channel_id=1, source_target_pairs={{0,4},{4,8},{8,12},{12,0},{16,20},{20,24},{24,28},{28,16},{32,36},... | collective-permute-start | bytes 1228808 | tf_op jit(solution)/shard_map/ppermute | solution.py:255
  13.0 11.0 %collective-permute-start.6 = (bf16[2,624,256]{2,1,0:T(8,128)(2,1)}, bf16[2,624,256]{2,1,0:T(8,128)(2,1)}, u32[]{:S(2)}, u32[]{:S(2)}) collective-permute-start(bf16[2,624,256]{2,1,0:T(8,128)(2,1)} %get-tuple-element.22), channel_id=1, source_target_pairs={{0,508},{4,0},{8,4},{12,8},{16,12},{20,16},{24,20},{28,24},{32,28}... | collective-permute-start | bytes 1916936 | tf_op jit(solution)/shard_map/ppermute | solution.py:256
  24.0 0.6 pad_add_fusion.1.seq_ref
  24.6 37.4 %collective-permute-done.1 = bf16[2,400,256]{2,1,0:T(8,128)(2,1)} collective-permute-done((bf16[2,400,256]{2,1,0:T(8,128)(2,1)}, bf16[2,400,256]{2,1,0:T(8,128)(2,1)}, u32[]{:S(2)}, u32[]{:S(2)}) %collective-permute-start.1) | collective-permute-done | bytes 409632 | tf_op jit(solution)/shard_map/ppermute | solution.py:255
  62.0 1.9 %collective-permute-start.4 = (bf16[2,400,256]{2,1,0:T(8,128)(2,1)}, bf16[2,400,256]{2,1,0:T(8,128)(2,1)S(1)}, u32[]{:S(2)}, u32[]{:S(2)}) collective-permute-start(bf16[2,400,256]{2,1,0:T(8,128)(2,1)} %collective-permute-done.1), channel_id=1, source_target_pairs={{0,4},{4,504},{8,508},{12,0},{16,20},{20,8},{24,12},{28,16},{32,36... | collective-permute-start | bytes 1228808 | tf_op jit(solution)/shard_map/ppermute | solution.py:260
  63.9 0.0 collective-permute-done.refs_2_
  63.9 3.5 %collective-permute-start.3 = (bf16[1024,512]{1,0:T(8,128)(2,1)}, bf16[1024,512]{1,0:T(8,128)(2,1)}, u32[]{:S(2)}, u32[]{:S(2)}) collective-permute-start(bf16[1024,512]{1,0:T(8,128)(2,1)} %collective-permute-done.refs_2_), channel_id=1, source_target_pairs={{0,1},{1,0},{2,3},{3,2},{4,5},{5,4},{6,7},{7,6},{8,9},{9,8},{10,11... | collective-permute-start | bytes 3145736 | tf_op jit(solution)/shard_map/ppermute | solution.py:259
  67.4 0.0 copy-done.2
  67.4 1.9 %collective-permute-start.2 = (bf16[1024,512]{1,0:T(8,128)(2,1)S(1)}, bf16[1024,512]{1,0:T(8,128)(2,1)}, u32[]{:S(2)}, u32[]{:S(2)}) collective-permute-start(bf16[1024,512]{1,0:T(8,128)(2,1)S(1)} %copy-done.2), channel_id=1, source_target_pairs={{0,1},{1,0},{2,3},{3,2},{4,5},{5,4},{6,7},{7,6},{8,9},{9,8},{10,11... | collective-permute-start | bytes 3145736 | tf_op jit(solution)/shard_map/ppermute | solution.py:258
  69.3 0.0 copy-start
  69.3 0.0 copy-start.1
  69.4 2.2 %shard_map.93 = (s32[1024,128]{1,0:T(8,128)}, s32[1024,128]{1,0:T(8,128)}) custom-call(s32[2]{0:T(128)} %pad_add_fusion.1.seq_ref, s32[16]{0:T(128)} %offset_ref.1, s32[16]{0:T(128)} %length_ref.1, s32[8,128]{1,0:T(8,128)} %bitcast.11), custom_call_target="tpu_custom_call" | custom-call | flops 20000000000 | bytes 1 | tf_op jit(solution)/shard_map/pallas_call | solution.py:92
  71.6 0.0 collective-permute-done.6.refs_0_
  71.6 10.8 %collective-permute-start.7 = (bf16[2,624,256]{2,1,0:T(8,128)(2,1)}, bf16[2,624,256]{2,1,0:T(8,128)(2,1)S(1)}, u32[]{:S(2)}, u32[]{:S(2)}) collective-permute-start(bf16[2,624,256]{2,1,0:T(8,128)(2,1)} %collective-permute-done.6.refs_0_), channel_id=1, source_target_pairs={{0,508},{4,0},{8,4},{12,8},{16,12},{20,16},{24,20},{28,24},{32,28}... | collective-permute-start | bytes 1916936 | tf_op jit(solution)/shard_map/ppermute | solution.py:261
  82.4 0.1 pad_add_fusion.order_ref
  82.5 0.0 copy-start.5
  82.5 0.0 copy-start.6
  82.5 0.0 copy-start.7
  82.5 0.0 copy-start.8
  82.5 0.0 collective-permute-done.2.refs_1_
  82.5 0.0 collective-permute-done.3.refs_3_
  82.5 0.0 copy-done
  82.5 0.0 copy-done.1
  82.5 5.1 %shard_map.92 = (bf16[1024,256]{1,0:T(8,128)(2,1)S(1)}, f32[1024,256]{1,0:T(8,128)S(1)}) custom-call(s32[4]{0:T(128)S(1)} %pad_add_fusion.order_ref, bf16[1024,512]{1,0:T(8,128)(2,1)S(1)} %copy-done.2, bf16[1024,512]{1,0:T(8,128)(2,1)} %collective-permute-done.2.refs_1_, bf16[1024,512]{1,0:T(8,128)(2,1)} %collective-permute-done.refs_2_, ...), custom_call_target="tpu_custom_call" | custom-call | flops 500000000 | bytes 1 | tf_op jit(solution)/shard_map/pallas_call | solution.py:123
  87.6 0.0 copy-start.3
  87.6 1.0 copy-done.3
  88.6 0.0 collective-permute-done.4.refs_0_
  88.6 1.9 %collective-permute-start.5 = (bf16[2,400,256]{2,1,0:T(8,128)(2,1)S(1)}, bf16[2,400,256]{2,1,0:T(8,128)(2,1)S(1)}, u32[]{:S(2)}, u32[]{:S(2)}) collective-permute-start(bf16[2,400,256]{2,1,0:T(8,128)(2,1)S(1)} %collective-permute-done.4.refs_0_), channel_id=1, source_target_pairs={{0,4},{4,8},{8,12},{12,16},{16,20},{20,24},{24,28},{28,32},{32,36}... | collective-permute-start | bytes 1228808 | tf_op jit(solution)/shard_map/ppermute | solution.py:266
  90.5 0.0 copy-done.5
  90.5 0.0 copy-done.6
  90.5 0.0 copy-done.7
  90.6 0.0 copy-done.8
  90.6 3.5 %shard_map.94.refs_1_ = f32[1024,256]{1,0:T(8,128)S(1)} custom-call(bf16[1024,256]{1,0:T(8,128)(2,1)S(1)} %get-tuple-element.19.query_ref, s32[1024,128]{1,0:T(8,128)S(1)} %copy-done.8, s32[1024,128]{1,0:T(8,128)S(1)} %copy-done.7, bf16[1024,256]{1,0:T(8,128)(2,1)S(1)} %copy-done.5, bf16[1024,256]{1,0:T(8,128)(2,1)S(1)} %copy-done.6), custom_call_target="tpu_custom_call" | custom-call | flops 1000000000 | bytes 1 | tf_op jit(solution)/shard_map/pallas_call | solution.py:199
  94.1 3.1 %shard_map.95.refs_1_ = f32[1024,256]{1,0:T(8,128)S(1)} custom-call(bf16[1024,256]{1,0:T(8,128)(2,1)S(1)} %get-tuple-element.19.query_ref, s32[1024,128]{1,0:T(8,128)S(1)} %copy-done.7, bf16[2,624,256]{2,1,0:T(8,128)(2,1)} %collective-permute-done.6.refs_0_, f32[1024,256]{1,0:T(8,128)S(1)} %shard_map.94.refs_1_), custom_call_target="tpu_custom_call", output_to_operand_aliasing={{}: (3, {})} | custom-call | flops 500000000 | bytes 1 | tf_op jit(solution)/shard_map/pallas_call | solution.py:215
  97.2 1.5 %shard_map.96.refs_1_ = f32[1024,256]{1,0:T(8,128)S(1)} custom-call(bf16[1024,256]{1,0:T(8,128)(2,1)S(1)} %get-tuple-element.19.query_ref, s32[1024,128]{1,0:T(8,128)S(1)} %copy-done.7, bf16[2,400,256]{2,1,0:T(8,128)(2,1)S(1)} %collective-permute-done.4.refs_0_, f32[1024,256]{1,0:T(8,128)S(1)} %shard_map.95.refs_1_), custom_call_target="tpu_custom_call", output_to_operand_aliasing={{}: (3, {})} | custom-call | flops 4000000000 | bytes 1 | tf_op jit(solution)/shard_map/pallas_call | solution.py:215
  98.7 0.0 collective-permute-done.7.refs_0_
  98.7 2.0 %shard_map.97.refs_1_ = f32[1024,256]{1,0:T(8,128)S(1)} custom-call(bf16[1024,256]{1,0:T(8,128)(2,1)S(1)} %get-tuple-element.19.query_ref, s32[1024,128]{1,0:T(8,128)S(1)} %copy-done.7, bf16[2,624,256]{2,1,0:T(8,128)(2,1)S(1)} %collective-permute-done.7.refs_0_, f32[1024,256]{1,0:T(8,128)S(1)} %shard_map.96.refs_1_), custom_call_target="tpu_custom_call", output_to_operand_aliasing={{}: (3, {})} | custom-call | flops 4000000000 | bytes 1 | tf_op jit(solution)/shard_map/pallas_call | solution.py:215
  100.8 0.0 copy-start.4
  100.8 6.3 %collective-permute-done.5.refs_0_ = bf16[2,400,256]{2,1,0:T(8,128)(2,1)S(1)} collective-permute-done((bf16[2,400,256]{2,1,0:T(8,128)(2,1)S(1)}, bf16[2,400,256]{2,1,0:T(8,128)(2,1)S(1)}, u32[]{:S(2)}, u32[]{:S(2)}) %collective-permute-start.5) | collective-permute-done | bytes 409632 | tf_op jit(solution)/shard_map/ppermute | solution.py:266
  107.0 1.6 %shard_map.98 = (f32[1024,256]{1,0:T(8,128)S(1)}, f32[2,1024]{1,0:T(2,128)S(1)}) custom-call(bf16[1024,256]{1,0:T(8,128)(2,1)S(1)} %get-tuple-element.19.query_ref, s32[1024,128]{1,0:T(8,128)S(1)} %copy-done.7, bf16[2,400,256]{2,1,0:T(8,128)(2,1)S(1)} %collective-permute-done.5.refs_0_, ...), custom_call_target="tpu_custom_call", output_to_operand_aliasing={{0}: (3, {})} | custom-call | flops 4000000000 | bytes 1 | tf_op jit(solution)/shard_map/pallas_call | solution.py:215
  108.6 6.8 %psum.7 = f32[2,1024]{1,0:T(2,128)S(1)} all-reduce(f32[2,1024]{1,0:T(2,128)S(1)} %get-tuple-element.25), channel_id=1, replica_groups=mesh['seq'=128,'tp'=4] {'tp'}, use_global_device_ids=true, to_apply=%region_0.0 | all-reduce | flops 2048 | bytes 16384 | tf_op jit(solution)/shard_map/psum | solution.py:273
  115.4 0.0 copy-start.9
  115.5 0.0 copy-done.4
  115.5 0.7 copy-done.9
  116.1 1.1 multiply_convert_fusion
  (3 shorter events, 0.0 us)
Async XLA Ops:
  0.0 67.4 %copy-start.2 = (bf16[1024,512]{1,0:T(8,128)(2,1)S(1)}, bf16[1024,512]{1,0:T(8,128)(2,1)}, u32[]{:S(2)}) copy-start(bf16[1024,512]{1,0:T(8,128)(2,1)} %refs_0_.1) | copy-start | bytes 3145732
  0.0 63.9 %collective-permute-start = (bf16[1024,512]{1,0:T(8,128)(2,1)}, bf16[1024,512]{1,0:T(8,128)(2,1)}, u32[]{:S(2)}, u32[]{:S(2)}) collective-permute-start(bf16[1024,512]{1,0:T(8,128)(2,1)} %refs_0_.1), channel_id=1, source_target_pairs={{0,2},{2,0},{1,3},{3,1},{4,6},{6,4},{5,7},{7,5},{8,10},{10,8},{9,1... | collective-permute-start | bytes 3145736 | tf_op jit(solution)/shard_map/ppermute | solution.py:254
  7.2 54.8 %collective-permute-start.1 = (bf16[2,400,256]{2,1,0:T(8,128)(2,1)}, bf16[2,400,256]{2,1,0:T(8,128)(2,1)}, u32[]{:S(2)}, u32[]{:S(2)}) collective-permute-start(bf16[2,400,256]{2,1,0:T(8,128)(2,1)} %get-tuple-element.16), channel_id=1, source_target_pairs={{0,4},{4,8},{8,12},{12,0},{16,20},{20,24},{24,28},{28,16},{32,36},... | collective-permute-start | bytes 1228808 | tf_op jit(solution)/shard_map/ppermute | solution.py:255
  13.0 58.6 %collective-permute-start.6 = (bf16[2,624,256]{2,1,0:T(8,128)(2,1)}, bf16[2,624,256]{2,1,0:T(8,128)(2,1)}, u32[]{:S(2)}, u32[]{:S(2)}) collective-permute-start(bf16[2,624,256]{2,1,0:T(8,128)(2,1)} %get-tuple-element.22), channel_id=1, source_target_pairs={{0,508},{4,0},{8,4},{12,8},{16,12},{20,16},{24,20},{28,24},{32,28}... | collective-permute-start | bytes 1916936 | tf_op jit(solution)/shard_map/ppermute | solution.py:256
  62.0 26.6 %collective-permute-start.4 = (bf16[2,400,256]{2,1,0:T(8,128)(2,1)}, bf16[2,400,256]{2,1,0:T(8,128)(2,1)S(1)}, u32[]{:S(2)}, u32[]{:S(2)}) collective-permute-start(bf16[2,400,256]{2,1,0:T(8,128)(2,1)} %collective-permute-done.1), channel_id=1, source_target_pairs={{0,4},{4,504},{8,508},{12,0},{16,20},{20,8},{24,12},{28,16},{32,36... | collective-permute-start | bytes 1228808 | tf_op jit(solution)/shard_map/ppermute | solution.py:260
  63.9 18.6 %collective-permute-start.3 = (bf16[1024,512]{1,0:T(8,128)(2,1)}, bf16[1024,512]{1,0:T(8,128)(2,1)}, u32[]{:S(2)}, u32[]{:S(2)}) collective-permute-start(bf16[1024,512]{1,0:T(8,128)(2,1)} %collective-permute-done.refs_2_), channel_id=1, source_target_pairs={{0,1},{1,0},{2,3},{3,2},{4,5},{5,4},{6,7},{7,6},{8,9},{9,8},{10,11... | collective-permute-start | bytes 3145736 | tf_op jit(solution)/shard_map/ppermute | solution.py:259
  67.4 15.1 %collective-permute-start.2 = (bf16[1024,512]{1,0:T(8,128)(2,1)S(1)}, bf16[1024,512]{1,0:T(8,128)(2,1)}, u32[]{:S(2)}, u32[]{:S(2)}) collective-permute-start(bf16[1024,512]{1,0:T(8,128)(2,1)S(1)} %copy-done.2), channel_id=1, source_target_pairs={{0,1},{1,0},{2,3},{3,2},{4,5},{5,4},{6,7},{7,6},{8,9},{9,8},{10,11... | collective-permute-start | bytes 3145736 | tf_op jit(solution)/shard_map/ppermute | solution.py:258
  69.3 13.2 %copy-start = (bf16[2048,256]{1,0:T(8,128)(2,1)S(1)}, bf16[2048,256]{1,0:T(8,128)(2,1)}, u32[]{:S(2)}) copy-start(bf16[2048,256]{1,0:T(8,128)(2,1)} %refs_7_.1) | copy-start | bytes 3145732
  69.3 13.2 %copy-start.1 = (bf16[2048,256]{1,0:T(8,128)(2,1)S(1)}, bf16[2048,256]{1,0:T(8,128)(2,1)}, u32[]{:S(2)}) copy-start(bf16[2048,256]{1,0:T(8,128)(2,1)} %refs_11_.1) | copy-start | bytes 3145732
  71.6 27.2 %collective-permute-start.7 = (bf16[2,624,256]{2,1,0:T(8,128)(2,1)}, bf16[2,624,256]{2,1,0:T(8,128)(2,1)S(1)}, u32[]{:S(2)}, u32[]{:S(2)}) collective-permute-start(bf16[2,624,256]{2,1,0:T(8,128)(2,1)} %collective-permute-done.6.refs_0_), channel_id=1, source_target_pairs={{0,508},{4,0},{8,4},{12,8},{16,12},{20,16},{24,20},{28,24},{32,28}... | collective-permute-start | bytes 1916936 | tf_op jit(solution)/shard_map/ppermute | solution.py:261
  82.5 8.1 %copy-start.5 = (bf16[1024,256]{1,0:T(8,128)(2,1)S(1)}, bf16[1024,256]{1,0:T(8,128)(2,1)}, u32[]{:S(2)}) copy-start(bf16[1024,256]{1,0:T(8,128)(2,1)} %key_ref.3) | copy-start | bytes 1572868
  82.5 8.1 %copy-start.6 = (bf16[1024,256]{1,0:T(8,128)(2,1)S(1)}, bf16[1024,256]{1,0:T(8,128)(2,1)}, u32[]{:S(2)}) copy-start(bf16[1024,256]{1,0:T(8,128)(2,1)} %value_ref.3) | copy-start | bytes 1572868
  82.5 8.1 %copy-start.7 = (s32[1024,128]{1,0:T(8,128)S(1)}, s32[1024,128]{1,0:T(8,128)}, u32[]{:S(2)}) copy-start(s32[1024,128]{1,0:T(8,128)} %get-tuple-element.20.end_ref) | copy-start | bytes 1572868
  82.5 8.1 %copy-start.8 = (s32[1024,128]{1,0:T(8,128)S(1)}, s32[1024,128]{1,0:T(8,128)}, u32[]{:S(2)}) copy-start(s32[1024,128]{1,0:T(8,128)} %get-tuple-element.23.start_ref) | copy-start | bytes 1572868
  87.6 1.0 copy-start.3
  88.6 18.4 %collective-permute-start.5 = (bf16[2,400,256]{2,1,0:T(8,128)(2,1)S(1)}, bf16[2,400,256]{2,1,0:T(8,128)(2,1)S(1)}, u32[]{:S(2)}, u32[]{:S(2)}) collective-permute-start(bf16[2,400,256]{2,1,0:T(8,128)(2,1)S(1)} %collective-permute-done.4.refs_0_), channel_id=1, source_target_pairs={{0,4},{4,8},{8,12},{12,16},{16,20},{20,24},{24,28},{28,32},{32,36}... | collective-permute-start | bytes 1228808 | tf_op jit(solution)/shard_map/ppermute | solution.py:266
  100.8 14.7 %copy-start.4 = (f32[1024,256]{1,0:T(8,128)S(1)}, f32[1024,256]{1,0:T(8,128)}, u32[]{:S(2)}) copy-start(f32[1024,256]{1,0:T(8,128)} %copy-done.3) | copy-start | bytes 3145732
  115.4 0.7 copy-start.9

commit v4 on v1

--- a/solution.py
+++ b/solution.py
@@ -12,9 +12,12 @@
 HQ = 1024
 Z_HI = 4
 LANES = 128
-DOWN_ROWS = 640
+DOWN = (672,)
+UP = (352,)
 VMEM = pl.BlockSpec(memory_space=pltpu.VMEM)
+HBM = pl.BlockSpec(memory_space=pltpu.HBM)
 SMEM = pl.BlockSpec(memory_space=pltpu.SMEM)
+FULL = pltpu.CompilerParams(vmem_limit_bytes=60 * 2**20)
 PARAMS = pltpu.CompilerParams(vmem_limit_bytes=40 * 2**20)
 
 
@@ -37,6 +40,32 @@
             pairs.append((i, target))
         up.append(pairs)
     return down, up
+
+
+def pack_kernel(chunks, key_ref, value_ref, *refs):
+    outs, sems = refs[:-1], refs[-1]
+    copies = []
+    for (at, size), out in zip(chunks, outs):
+        for place, ref in enumerate((key_ref, value_ref)):
+            copies.append(
+                pltpu.make_async_copy(ref.at[pl.ds(at, size)], out.at[place], sems.at[len(copies)])
+            )
+    for copy in copies:
+        copy.start()
+    for copy in copies:
+        copy.wait()
+
+
+def pack(keys, values, chunks):
+    width = keys.shape[1]
+    return pl.pallas_call(
+        functools.partial(pack_kernel, chunks),
+        out_shape=[jax.ShapeDtypeStruct((2, size, width), keys.dtype) for _, size in chunks],
+        in_specs=[HBM] * 2,
+        out_specs=[VMEM] * len(chunks),
+        scratch_shapes=[pltpu.SemaphoreType.DMA((2 * len(chunks),))],
+        compiler_params=FULL,
+    )(keys, values)
 
 
 def windows_kernel(seq_ref, offset_ref, length_ref, user_ref, start_ref, end_ref):
@@ -114,7 +143,7 @@
         ),
         compiler_params=PARAMS,
         cost_estimate=pl.CostEstimate(
-            flops=8 * rows * depth * width, bytes_accessed=8 * rows * depth, transcendentals=0
+            flops=80 * rows * depth * width // 10, bytes_accessed=8 * rows * depth, transcendentals=0
         ),
     )(order, *args)
 
@@ -128,12 +157,13 @@
         )
         columns = []
         for lane in range(0, size, LANES):
-            half = scores[:, lane : lane + LANES] * (0.5 * HDIM**-0.5)
+            lanes = min(LANES, size - lane)
+            half = scores[:, lane : lane + lanes] * (0.5 * HDIM**-0.5)
             weight = half * jnp.tanh(half) + half
-            position = lax.broadcasted_iota(jnp.int32, (rows, LANES), 1) + (place + at + lane)
-            inside = position < end
+            position = lax.broadcasted_iota(jnp.int32, (rows, lanes), 1) + (place + at + lane)
+            inside = position < end[:, :lanes]
             if start is not None:
-                inside = inside & (position >= start)
+                inside = inside & (position >= start[:, :lanes])
             columns.append(jnp.where(inside, weight, 0.0).astype(jnp.bfloat16))
         total = total + jnp.dot(
             jnp.concatenate(columns, axis=1), values[at : at + size], preferred_element_type=jnp.float32
@@ -150,14 +180,16 @@
         )
 
 
-def next_kernel(query_ref, end_ref, pair_ref, total_ref, out_ref, *stats, place):
+def next_kernel(query_ref, end_ref, *refs, places):
+    pairs, (total_ref, out_ref, *stats) = refs[: len(places)], refs[len(places) :]
     parts = []
     for head in range(query_ref.shape[1] // HDIM):
         cols = slice(head * HDIM, (head + 1) * HDIM)
-        part = weigh(
-            query_ref[:, cols], pair_ref[0, :, cols], pair_ref[1, :, cols], None, end_ref[...], place,
-            total_ref[:, cols],
-        )
+        part = total_ref[:, cols]
+        for place, pair_ref in zip(places, pairs):
+            part = weigh(
+                query_ref[:, cols], pair_ref[0, :, cols], pair_ref[1, :, cols], None, end_ref[...], place, part
+            )
         out_ref[:, cols] = part
         parts.append(part)
     if stats:
@@ -172,7 +204,7 @@
 
 def attend_cost(rows, history, width):
     return pl.CostEstimate(
-        flops=4 * rows * history * width, bytes_accessed=8 * rows * width, transcendentals=rows * history * 2
+        flops=20 * rows * history * width // 10, bytes_accessed=8 * rows * width, transcendentals=rows * history * 2
     )
 
 
@@ -187,20 +219,26 @@
     )(query, start, end, keys, values)
 
 
-def attend_next(query, end, pair, total, place, last=False):
+def attend_next(query, end, chunks, total, last=False):
+    pairs, places = zip(*chunks)
     out_shape = [jax.ShapeDtypeStruct(query.shape, jnp.float32)]
     if last:
         out_shape.append(jax.ShapeDtypeStruct((2, query.shape[0]), jnp.float32))
+    history = sum(pair.shape[1] for pair in pairs)
     out = pl.pallas_call(
-        functools.partial(next_kernel, place=place),
+        functools.partial(next_kernel, places=places),
         out_shape=out_shape,
-        in_specs=[VMEM] * 4,
+        in_specs=[VMEM] * (3 + len(pairs)),
         out_specs=[VMEM] * len(out_shape),
-        input_output_aliases={3: 0},
+        input_output_aliases={2 + len(pairs): 0},
         compiler_params=PARAMS,
-        cost_estimate=attend_cost(query.shape[0], *pair.shape[1:]),
-    )(query, end, pair, total)
+        cost_estimate=attend_cost(query.shape[0], history, query.shape[1]),
+    )(query, end, *pairs, total)
     return out if last else out[0]
+
+
+def after(array, *others):
+    return lax.optimization_barrier((array, *others))[0]
 
 
 def body(
@@ -216,32 +254,33 @@
 ):
     hist_rows = hist_keys.shape[0]
     down, up = ring_perms(lax.axis_size("seq"))
-    cut = DOWN_ROWS
     other_chip = [(0, 2), (2, 0), (1, 3), (3, 1)]
     other_core = [(0, 1), (1, 0), (2, 3), (3, 2)]
-
-    pair_a = jnp.stack([hist_keys[:cut], hist_values[:cut]])
-    pair_b = jnp.stack([hist_keys[cut:], hist_values[cut:]])
+    sizes = DOWN + UP
+    at = [sum(sizes[:i]) for i in range(len(sizes))]
+    chunks = tuple(zip(at, sizes))
+
+    near = lax.ppermute(targets, "tp", other_core)
+    a, b = pack(hist_keys, hist_values, chunks)
     far = lax.ppermute(targets, "tp", other_chip)
-    next_a = lax.ppermute(pair_a, "seq", down)
-    up_b = lax.ppermute(pair_b, "seq", up[0])
-    near = lax.ppermute(targets, "tp", other_core)
-    far_near = lax.ppermute(far, "tp", other_core)
-    over_b = lax.ppermute(up_b, "seq", up[1])
-    over_a = lax.ppermute(next_a, "seq", down)
-    next_b = lax.ppermute(over_b, "seq", up[2])
-
+    a1 = lax.ppermute(a, "seq", down)
+    b1 = lax.ppermute(b, "seq", up[0])
     me = lax.axis_index("tp").astype(jnp.int32)
     seq_info = jnp.stack([lax.axis_index("seq").astype(jnp.int32), jnp.int32(hist_rows)])
     start, end = windows(seq_info, user_offset, user_length, target_user)
     partial = project(jnp.stack([me, me ^ 1]), targets, near, w_query, w_gate)
+    far, b1 = lax.optimization_barrier((far, b1))
+    far_near = lax.ppermute(far, "tp", other_core)
+    b2 = lax.ppermute(b1, "seq", up[1])
+    a2 = lax.ppermute(a1, "seq", down)
     query, gate = project(jnp.stack([me ^ 2, me ^ 3]), far, far_near, w_query, w_gate, partial)
-
     total = attend_own(query, start, end, hist_keys, hist_values)
-    total = attend_next(query, end, next_a, total, hist_rows)
-    total = attend_next(query, end, over_b, total, 2 * hist_rows + cut)
-    total = attend_next(query, end, over_a, total, 2 * hist_rows)
-    attended, stats = attend_next(query, end, next_b, total, hist_rows + cut, last=True)
+    b3 = lax.ppermute(b2, "seq", up[2])
+    one, two = hist_rows, 2 * hist_rows
+    total = attend_next(query, end, [(a1, one + at[0])], total)
+    total = attend_next(query, end, [(b2, two + at[1])], total)
+    total = attend_next(query, end, [(a2, two + at[0])], total)
+    attended, stats = attend_next(query, end, [(b3, one + at[1])], total, last=True)
 
     sums = lax.psum(stats, "tp") / HQ
     mean = sums[0]

time: 145 us -> 116 us (0.80)
  the two profiles are of different devices: /device:TPU:186 before, /device:TPU:1 now
where the time goes in v4:
time: 116 us; the launch traced here: 114 us
  starting transfers between devices  42.1 us (36%)
  waiting for transfers between devices  36.9 us (32%)
  Pallas kernels  20.9 us (18%)
  blocking collectives  7.1 us (6%)
  local copies, waits for them, and re-layouts  5.7 us (5%)
  other arithmetic  1.38 us (1%)
    ppermute x1, waiting for transfers between devices, body(): b1 = lax.ppermute(b, 'seq', up[0])  24 us
    ppermute x1, waiting for transfers between devices, body(): b2 = lax.ppermute(b1, 'seq', up[1])  11.6 us
    ppermute x1, starting transfers between devices, body(): a1 = lax.ppermute(a, 'seq', down)  11 us
    pallas_call x4, Pallas kernels, attend_next(): pl.pallas_call(functools.partial(next_kernel, places=places), out_shape=o...  9.53 us
    ppermute x1, starting transfers between devices, body(): far_near = lax.ppermute(far, 'tp', other_core)  8.23 us
    psum x1, blocking collectives, body(): sums = lax.psum(stats, 'tp') / HQ  7.1 us
    ppermute x1, starting transfers between devices, body(): b1 = lax.ppermute(b, 'seq', up[0])  5.81 us
    unnamed x22, local copies, waits for them, and re-layouts  5.69 us
  transfers between devices with their start and end apart: 8, of which 3 were waited for; matrix products, arithmetic and copies ran while one was open for 0% of the time, Pallas kernels for 17%

profile of v4, /device:TPU:1, one launch (start us, length us, event | category | flops | bytes accessed | tf_op | source)
XLA Modules:
  0.0 114.3 jit_solution(1488756674140868340)
XLA Ops:
  0.0 4.8 %collective-permute-start = (bf16[1024,512]{1,0:T(8,128)(2,1)}, bf16[1024,512]{1,0:T(8,128)(2,1)S(1)}, u32[]{:S(2)}, u32[]{:S(2)}) collective-permute-start(bf16[1024,512]{1,0:T(8,128)(2,1)} %a_ref.1), channel_id=1, source_target_pairs={{0,2},{2,0},{1,3},{3,1},{4,6},{6,4},{5,7},{7,5},{8,10},{10,8},{9,1... | collective-permute-start | bytes 3145736 | tf_op jit(solution)/shard_map/ppermute | solution.py:265
  4.8 2.2 %shard_map.91 = (bf16[2,672,256]{2,1,0:T(8,128)(2,1)}, bf16[2,352,256]{2,1,0:T(8,128)(2,1)}) custom-call(bf16[1024,256]{1,0:T(8,128)(2,1)} %key_ref.3, bf16[1024,256]{1,0:T(8,128)(2,1)} %value_ref.3), custom_call_target="tpu_custom_call" | custom-call | tf_op jit(solution)/shard_map/pallas_call | solution.py:61
  7.0 5.8 %collective-permute-start.1 = (bf16[2,352,256]{2,1,0:T(8,128)(2,1)}, bf16[2,352,256]{2,1,0:T(8,128)(2,1)}, u32[]{:S(2)}, u32[]{:S(2)}) collective-permute-start(bf16[2,352,256]{2,1,0:T(8,128)(2,1)} %get-tuple-element.15), channel_id=1, source_target_pairs={{0,4},{4,8},{8,12},{12,0},{16,20},{20,24},{24,28},{28,16},{32,36},... | collective-permute-start | bytes 1081352 | tf_op jit(solution)/shard_map/ppermute | solution.py:267
  12.8 11.0 %collective-permute-start.6 = (bf16[2,672,256]{2,1,0:T(8,128)(2,1)}, bf16[2,672,256]{2,1,0:T(8,128)(2,1)}, u32[]{:S(2)}, u32[]{:S(2)}) collective-permute-start(bf16[2,672,256]{2,1,0:T(8,128)(2,1)} %get-tuple-element.20), channel_id=1, source_target_pairs={{0,508},{4,0},{8,4},{12,8},{16,12},{20,16},{24,20},{28,24},{32,28}... | collective-permute-start | bytes 2064392 | tf_op jit(solution)/shard_map/ppermute | solution.py:266
  23.8 3.1 %collective-permute-start.3 = (bf16[1024,512]{1,0:T(8,128)(2,1)}, bf16[1024,512]{1,0:T(8,128)(2,1)S(1)}, u32[]{:S(2)}, u32[]{:S(2)}) collective-permute-start(bf16[1024,512]{1,0:T(8,128)(2,1)} %a_ref.1), channel_id=1, source_target_pairs={{0,1},{1,0},{2,3},{3,2},{4,5},{5,4},{6,7},{7,6},{8,9},{9,8},{10,11... | collective-permute-start | bytes 3145736 | tf_op jit(solution)/shard_map/ppermute | solution.py:263
  27.0 24.0 %collective-permute-done.1 = bf16[2,352,256]{2,1,0:T(8,128)(2,1)} collective-permute-done((bf16[2,352,256]{2,1,0:T(8,128)(2,1)}, bf16[2,352,256]{2,1,0:T(8,128)(2,1)}, u32[]{:S(2)}, u32[]{:S(2)}) %collective-permute-start.1) | collective-permute-done | bytes 360480 | tf_op jit(solution)/shard_map/ppermute | solution.py:267
  51.0 1.3 %collective-permute-done.a_ref = bf16[1024,512]{1,0:T(8,128)(2,1)S(1)} collective-permute-done((bf16[1024,512]{1,0:T(8,128)(2,1)}, bf16[1024,512]{1,0:T(8,128)(2,1)S(1)}, u32[]{:S(2)}, u32[]{:S(2)}) %collective-permute-start) | collective-permute-done | bytes 1048608 | tf_op jit(solution)/shard_map/ppermute | solution.py:265
  52.3 8.2 %collective-permute-start.2 = (bf16[1024,512]{1,0:T(8,128)(2,1)S(1)}, bf16[1024,512]{1,0:T(8,128)(2,1)S(1)}, u32[]{:S(2)}, u32[]{:S(2)}) collective-permute-start(bf16[1024,512]{1,0:T(8,128)(2,1)S(1)} %collective-permute-done.a_ref), channel_id=1, source_target_pairs={{0,1},{1,0},{2,3},{3,2},{4,5},{5,4},{6,7},{7,6},{8,9},{9,8},{10,11... | collective-permute-start | bytes 3145736 | tf_op jit(solution)/shard_map/ppermute | solution.py:273
  60.5 1.9 %collective-permute-start.4 = (bf16[2,352,256]{2,1,0:T(8,128)(2,1)}, bf16[2,352,256]{2,1,0:T(8,128)(2,1)S(1)}, u32[]{:S(2)}, u32[]{:S(2)}) collective-permute-start(bf16[2,352,256]{2,1,0:T(8,128)(2,1)} %collective-permute-done.1), channel_id=1, source_target_pairs={{0,4},{4,504},{8,508},{12,0},{16,20},{20,8},{24,12},{28,16},{32,36... | collective-permute-start | bytes 1081352 | tf_op jit(solution)/shard_map/ppermute | solution.py:274
  62.5 0.0 collective-permute-done.6.refs_0_
  62.5 4.5 %collective-permute-start.7 = (bf16[2,672,256]{2,1,0:T(8,128)(2,1)}, bf16[2,672,256]{2,1,0:T(8,128)(2,1)}, u32[]{:S(2)}, u32[]{:S(2)}) collective-permute-start(bf16[2,672,256]{2,1,0:T(8,128)(2,1)} %collective-permute-done.6.refs_0_), channel_id=1, source_target_pairs={{0,508},{4,0},{8,4},{12,8},{16,12},{20,16},{24,20},{28,24},{32,28}... | collective-permute-start | bytes 2064392 | tf_op jit(solution)/shard_map/ppermute | solution.py:275
  67.0 0.1 pad_add_fusion.1.order_ref
  67.0 0.1 pad_add_fusion.order_ref
  67.1 11.6 %collective-permute-done.4.refs_0_ = bf16[2,352,256]{2,1,0:T(8,128)(2,1)S(1)} collective-permute-done((bf16[2,352,256]{2,1,0:T(8,128)(2,1)}, bf16[2,352,256]{2,1,0:T(8,128)(2,1)S(1)}, u32[]{:S(2)}, u32[]{:S(2)}) %collective-permute-start.4) | collective-permute-done | bytes 360480 | tf_op jit(solution)/shard_map/ppermute | solution.py:274
  78.7 2.7 %collective-permute-start.5 = (bf16[2,352,256]{2,1,0:T(8,128)(2,1)S(1)}, bf16[2,352,256]{2,1,0:T(8,128)(2,1)S(1)}, u32[]{:S(2)}, u32[]{:S(2)}) collective-permute-start(bf16[2,352,256]{2,1,0:T(8,128)(2,1)S(1)} %collective-permute-done.4.refs_0_), channel_id=1, source_target_pairs={{0,4},{4,8},{8,12},{12,16},{16,20},{20,24},{24,28},{28,32},{32,36}... | collective-permute-start | bytes 1081352 | tf_op jit(solution)/shard_map/ppermute | solution.py:278
  81.4 0.1 pad_add_fusion.2.seq_ref
  81.5 0.0 copy-start.7
  81.5 0.7 copy-done.7
  82.1 0.0 copy-start.8
  82.1 0.7 copy-done.8
  82.8 0.0 copy-start.9
  82.8 0.7 copy-done.9
  83.5 0.9 shard_map.94
  84.4 0.0 collective-permute-done.3.b_ref
  84.4 0.0 copy-start
  84.4 1.2 %copy-done = bf16[2048,256]{1,0:T(8,128)(2,1)S(1)} copy-done((bf16[2048,256]{1,0:T(8,128)(2,1)S(1)}, bf16[2048,256]{1,0:T(8,128)(2,1)}, u32[]{:S(2)}) %copy-start) | copy-done | bytes 1048600
  85.6 0.0 copy-start.2
  85.6 1.2 %copy-done.2 = bf16[2048,256]{1,0:T(8,128)(2,1)S(1)} copy-done((bf16[2048,256]{1,0:T(8,128)(2,1)S(1)}, bf16[2048,256]{1,0:T(8,128)(2,1)}, u32[]{:S(2)}) %copy-start.2) | copy-done | bytes 1048600
  86.8 0.0 copy-start.4
  86.8 1.2 %copy-done.4 = bf16[1024,512]{1,0:T(8,128)(2,1)S(1)} copy-done((bf16[1024,512]{1,0:T(8,128)(2,1)S(1)}, bf16[1024,512]{1,0:T(8,128)(2,1)}, u32[]{:S(2)}) %copy-start.4) | copy-done | bytes 1048600
  88.1 0.0 copy-start.1
  88.1 0.0 copy-start.3
  88.1 2.3 %shard_map.92.refs_0_ = f32[1024,512]{1,0:T(8,128)S(1)} custom-call(s32[2]{0:T(128)S(1)} %pad_add_fusion.1.order_ref, bf16[1024,512]{1,0:T(8,128)(2,1)S(1)} %copy-done.4, bf16[1024,512]{1,0:T(8,128)(2,1)S(1)} %collective-permute-done.3.b_ref, bf16[2048,256]{1,0:T(8,128)(2,1)S(1)} %copy-done, bf16[2048,256]{1,0:T(8,128)(2,1)S(1)} %copy-done, ...), custom_call_target="tpu_custom_call" | custom-call | flops 1073741824 | bytes 4194304 | tf_op jit(solution)/shard_map/pallas_call | solution.py:138
  90.4 0.0 copy-start.5
  90.4 0.0 copy-start.6
  90.4 0.0 collective-permute-done.2.b_ref
  90.4 0.0 copy-done.1
  90.5 0.0 copy-done.3
  90.5 2.4 %shard_map.93 = (bf16[1024,256]{1,0:T(8,128)(2,1)S(1)}, f32[1024,256]{1,0:T(8,128)S(1)}) custom-call(s32[2]{0:T(128)S(1)} %pad_add_fusion.order_ref, bf16[1024,512]{1,0:T(8,128)(2,1)S(1)} %collective-permute-done.a_ref, bf16[1024,512]{1,0:T(8,128)(2,1)S(1)} %collective-permute-done.2.b_ref, bf16[2048,256]{1,0:T(8,128)(2,1)S(1)} %copy-done.1, ...), custom_call_target="tpu_custom_call" | custom-call | flops 1073741824 | bytes 4194304 | tf_op jit(solution)/shard_map/pallas_call | solution.py:138
  92.9 0.0 copy-done.5
  92.9 0.0 copy-done.6
  92.9 3.5 %shard_map.95.refs_1_ = f32[1024,256]{1,0:T(8,128)S(1)} custom-call(bf16[1024,256]{1,0:T(8,128)(2,1)S(1)} %get-tuple-element.17.query_ref, s32[1024,128]{1,0:T(8,128)S(1)} %get-tuple-element.21.start_ref, s32[1024,128]{1,0:T(8,128)S(1)} %get-tuple-element.18.end_ref, bf16[1024,256]{1,0:T(8,128)(2,1)S(1)} %copy-done.5, bf16[1024,256]{1,0:T(8,128)(2,1)S(1)} %copy-done.6), custom_call_target="tpu_custom_call" | custom-call | flops 536870912 | bytes 2097152 | tf_op jit(solution)/shard_map/pallas_call | solution.py:212
  96.4 3.1 %shard_map.96.refs_1_ = f32[1024,256]{1,0:T(8,128)S(1)} custom-call(bf16[1024,256]{1,0:T(8,128)(2,1)S(1)} %get-tuple-element.17.query_ref, s32[1024,128]{1,0:T(8,128)S(1)} %get-tuple-element.18.end_ref, bf16[2,672,256]{2,1,0:T(8,128)(2,1)} %collective-permute-done.6.refs_0_, f32[1024,256]{1,0:T(8,128)S(1)} %shard_map.95.refs_1_), custom_call_target="tpu_custom_call", output_to_operand_aliasing={{}: (3, {})} | custom-call | flops 352321536 | bytes 2097152 | tf_op jit(solution)/shard_map/pallas_call | solution.py:228
  99.6 1.5 %shard_map.97.refs_1_ = f32[1024,256]{1,0:T(8,128)S(1)} custom-call(bf16[1024,256]{1,0:T(8,128)(2,1)S(1)} %get-tuple-element.17.query_ref, s32[1024,128]{1,0:T(8,128)S(1)} %get-tuple-element.18.end_ref, bf16[2,352,256]{2,1,0:T(8,128)(2,1)S(1)} %collective-permute-done.4.refs_0_, f32[1024,256]{1,0:T(8,128)S(1)} %shard_map.96.refs_1_), custom_call_target="tpu_custom_call", output_to_operand_aliasing={{}: (3, {})} | custom-call | flops 184549376 | bytes 2097152 | tf_op jit(solution)/shard_map/pallas_call | solution.py:228
  101.1 0.0 collective-permute-done.7.refs_0_
  101.1 3.1 %shard_map.98.refs_1_ = f32[1024,256]{1,0:T(8,128)S(1)} custom-call(bf16[1024,256]{1,0:T(8,128)(2,1)S(1)} %get-tuple-element.17.query_ref, s32[1024,128]{1,0:T(8,128)S(1)} %get-tuple-element.18.end_ref, bf16[2,672,256]{2,1,0:T(8,128)(2,1)} %collective-permute-done.7.refs_0_, f32[1024,256]{1,0:T(8,128)S(1)} %shard_map.97.refs_1_), custom_call_target="tpu_custom_call", output_to_operand_aliasing={{}: (3, {})} | custom-call | flops 352321536 | bytes 2097152 | tf_op jit(solution)/shard_map/pallas_call | solution.py:228
  104.2 0.0 copy-start.10
  104.2 0.0 collective-permute-done.5.refs_0_
  104.2 1.8 %shard_map.99 = (f32[1024,256]{1,0:T(8,128)S(1)}, f32[2,1024]{1,0:T(2,128)S(1)}) custom-call(bf16[1024,256]{1,0:T(8,128)(2,1)S(1)} %get-tuple-element.17.query_ref, s32[1024,128]{1,0:T(8,128)S(1)} %get-tuple-element.18.end_ref, bf16[2,352,256]{2,1,0:T(8,128)(2,1)S(1)} %collective-permute-done.5.refs_0_, ...), custom_call_target="tpu_custom_call", output_to_operand_aliasing={{0}: (3, {})} | custom-call | flops 184549376 | bytes 2097152 | tf_op jit(solution)/shard_map/pallas_call | solution.py:228
  106.0 7.1 %psum.7 = f32[2,1024]{1,0:T(2,128)S(1)} all-reduce(f32[2,1024]{1,0:T(2,128)S(1)} %get-tuple-element.23), channel_id=1, replica_groups=mesh['seq'=128,'tp'=4] {'tp'}, use_global_device_ids=true, to_apply=%region_0.0 | all-reduce | flops 2048 | bytes 16384 | tf_op jit(solution)/shard_map/psum | solution.py:285
  113.2 0.0 copy-done.10
  113.2 1.1 multiply_convert_fusion
  (3 shorter events, 0.0 us)
Async XLA Ops:
  0.0 52.3 %collective-permute-start = (bf16[1024,512]{1,0:T(8,128)(2,1)}, bf16[1024,512]{1,0:T(8,128)(2,1)S(1)}, u32[]{:S(2)}, u32[]{:S(2)}) collective-permute-start(bf16[1024,512]{1,0:T(8,128)(2,1)} %a_ref.1), channel_id=1, source_target_pairs={{0,2},{2,0},{1,3},{3,1},{4,6},{6,4},{5,7},{7,5},{8,10},{10,8},{9,1... | collective-permute-start | bytes 3145736 | tf_op jit(solution)/shard_map/ppermute | solution.py:265
  7.0 44.0 %collective-permute-start.1 = (bf16[2,352,256]{2,1,0:T(8,128)(2,1)}, bf16[2,352,256]{2,1,0:T(8,128)(2,1)}, u32[]{:S(2)}, u32[]{:S(2)}) collective-permute-start(bf16[2,352,256]{2,1,0:T(8,128)(2,1)} %get-tuple-element.15), channel_id=1, source_target_pairs={{0,4},{4,8},{8,12},{12,0},{16,20},{20,24},{24,28},{28,16},{32,36},... | collective-permute-start | bytes 1081352 | tf_op jit(solution)/shard_map/ppermute | solution.py:267
  12.8 49.6 %collective-permute-start.6 = (bf16[2,672,256]{2,1,0:T(8,128)(2,1)}, bf16[2,672,256]{2,1,0:T(8,128)(2,1)}, u32[]{:S(2)}, u32[]{:S(2)}) collective-permute-start(bf16[2,672,256]{2,1,0:T(8,128)(2,1)} %get-tuple-element.20), channel_id=1, source_target_pairs={{0,508},{4,0},{8,4},{12,8},{16,12},{20,16},{24,20},{28,24},{32,28}... | collective-permute-start | bytes 2064392 | tf_op jit(solution)/shard_map/ppermute | solution.py:266
  23.8 60.6 %collective-permute-start.3 = (bf16[1024,512]{1,0:T(8,128)(2,1)}, bf16[1024,512]{1,0:T(8,128)(2,1)S(1)}, u32[]{:S(2)}, u32[]{:S(2)}) collective-permute-start(bf16[1024,512]{1,0:T(8,128)(2,1)} %a_ref.1), channel_id=1, source_target_pairs={{0,1},{1,0},{2,3},{3,2},{4,5},{5,4},{6,7},{7,6},{8,9},{9,8},{10,11... | collective-permute-start | bytes 3145736 | tf_op jit(solution)/shard_map/ppermute | solution.py:263
  52.3 38.1 %collective-permute-start.2 = (bf16[1024,512]{1,0:T(8,128)(2,1)S(1)}, bf16[1024,512]{1,0:T(8,128)(2,1)S(1)}, u32[]{:S(2)}, u32[]{:S(2)}) collective-permute-start(bf16[1024,512]{1,0:T(8,128)(2,1)S(1)} %collective-permute-done.a_ref), channel_id=1, source_target_pairs={{0,1},{1,0},{2,3},{3,2},{4,5},{5,4},{6,7},{7,6},{8,9},{9,8},{10,11... | collective-permute-start | bytes 3145736 | tf_op jit(solution)/shard_map/ppermute | solution.py:273
  60.5 18.1 %collective-permute-start.4 = (bf16[2,352,256]{2,1,0:T(8,128)(2,1)}, bf16[2,352,256]{2,1,0:T(8,128)(2,1)S(1)}, u32[]{:S(2)}, u32[]{:S(2)}) collective-permute-start(bf16[2,352,256]{2,1,0:T(8,128)(2,1)} %collective-permute-done.1), channel_id=1, source_target_pairs={{0,4},{4,504},{8,508},{12,0},{16,20},{20,8},{24,12},{28,16},{32,36... | collective-permute-start | bytes 1081352 | tf_op jit(solution)/shard_map/ppermute | solution.py:274
  62.5 38.6 %collective-permute-start.7 = (bf16[2,672,256]{2,1,0:T(8,128)(2,1)}, bf16[2,672,256]{2,1,0:T(8,128)(2,1)}, u32[]{:S(2)}, u32[]{:S(2)}) collective-permute-start(bf16[2,672,256]{2,1,0:T(8,128)(2,1)} %collective-permute-done.6.refs_0_), channel_id=1, source_target_pairs={{0,508},{4,0},{8,4},{12,8},{16,12},{20,16},{24,20},{28,24},{32,28}... | collective-permute-start | bytes 2064392 | tf_op jit(solution)/shard_map/ppermute | solution.py:275
  78.7 25.6 %collective-permute-start.5 = (bf16[2,352,256]{2,1,0:T(8,128)(2,1)S(1)}, bf16[2,352,256]{2,1,0:T(8,128)(2,1)S(1)}, u32[]{:S(2)}, u32[]{:S(2)}) collective-permute-start(bf16[2,352,256]{2,1,0:T(8,128)(2,1)S(1)} %collective-permute-done.4.refs_0_), channel_id=1, source_target_pairs={{0,4},{4,8},{8,12},{12,16},{16,20},{20,24},{24,28},{28,32},{32,36}... | collective-permute-start | bytes 1081352 | tf_op jit(solution)/shard_map/ppermute | solution.py:278
  81.5 0.7 copy-start.7
  82.1 0.7 copy-start.8
  82.8 0.7 copy-start.9
  84.4 1.2 %copy-start = (bf16[2048,256]{1,0:T(8,128)(2,1)S(1)}, bf16[2048,256]{1,0:T(8,128)(2,1)}, u32[]{:S(2)}) copy-start(bf16[2048,256]{1,0:T(8,128)(2,1)} %wqb.3) | copy-start | bytes 3145732
  85.6 1.2 %copy-start.2 = (bf16[2048,256]{1,0:T(8,128)(2,1)S(1)}, bf16[2048,256]{1,0:T(8,128)(2,1)}, u32[]{:S(2)}) copy-start(bf16[2048,256]{1,0:T(8,128)(2,1)} %wgb.3) | copy-start | bytes 3145732
  86.8 1.2 %copy-start.4 = (bf16[1024,512]{1,0:T(8,128)(2,1)S(1)}, bf16[1024,512]{1,0:T(8,128)(2,1)}, u32[]{:S(2)}) copy-start(bf16[1024,512]{1,0:T(8,128)(2,1)} %a_ref.1) | copy-start | bytes 3145732
  88.1 2.4 %copy-start.1 = (bf16[2048,256]{1,0:T(8,128)(2,1)S(1)}, bf16[2048,256]{1,0:T(8,128)(2,1)}, u32[]{:S(2)}) copy-start(bf16[2048,256]{1,0:T(8,128)(2,1)} %wqb.3) | copy-start | bytes 3145732
  88.1 2.4 %copy-start.3 = (bf16[2048,256]{1,0:T(8,128)(2,1)S(1)}, bf16[2048,256]{1,0:T(8,128)(2,1)}, u32[]{:S(2)}) copy-start(bf16[2048,256]{1,0:T(8,128)(2,1)} %wgb.3) | copy-start | bytes 3145732
  90.4 2.5 %copy-start.5 = (bf16[1024,256]{1,0:T(8,128)(2,1)S(1)}, bf16[1024,256]{1,0:T(8,128)(2,1)}, u32[]{:S(2)}) copy-start(bf16[1024,256]{1,0:T(8,128)(2,1)} %key_ref.3) | copy-start | bytes 1572868
  90.4 2.5 %copy-start.6 = (bf16[1024,256]{1,0:T(8,128)(2,1)S(1)}, bf16[1024,256]{1,0:T(8,128)(2,1)}, u32[]{:S(2)}) copy-start(bf16[1024,256]{1,0:T(8,128)(2,1)} %value_ref.3) | copy-start | bytes 1572868
  104.2 9.0 %copy-start.10 = (f32[256]{0:T(256)S(1)}, f32[256]{0:T(256)}, u32[]{:S(2)}) copy-start(f32[256]{0:T(256)} %param.12) | copy-start | bytes 3076

commit v5 on v4

--- a/solution.py
+++ b/solution.py
@@ -12,8 +12,8 @@
 HQ = 1024
 Z_HI = 4
 LANES = 128
-DOWN = (672,)
-UP = (352,)
+DOWN = (688,)
+UP = (336,)
 VMEM = pl.BlockSpec(memory_space=pltpu.VMEM)
 HBM = pl.BlockSpec(memory_space=pltpu.HBM)
 SMEM = pl.BlockSpec(memory_space=pltpu.SMEM)

time: 116 us -> 116 us (level)
  starting transfers between devices: 42.1 us -> 40.6 us
  waiting for transfers between devices: 36.9 us -> 38.1 us
    ppermute x1, starting transfers between devices: 4.48 us -> 3.07 us  [body(): a2 = lax.ppermute(a1, 'seq', down)]
    ppermute x1, waiting for transfers between devices: 1.31 us -> 2.72 us  [body(): far = lax.ppermute(targets, 'tp', other_chip)]
where the time goes in v5:
time: 116 us; the launch traced here: 114 us
  starting transfers between devices  40.6 us (35%)
  waiting for transfers between devices  38.1 us (33%)
  Pallas kernels  20.9 us (18%)
  blocking collectives  7.31 us (6%)
  local copies, waits for them, and re-layouts  5.7 us (5%)
  other arithmetic  1.38 us (1%)
    ppermute x1, waiting for transfers between devices, body(): b1 = lax.ppermute(b, 'seq', up[0])  23.3 us
    ppermute x1, waiting for transfers between devices, body(): b2 = lax.ppermute(b1, 'seq', up[1])  12.1 us
    ppermute x1, starting transfers between devices, body(): a1 = lax.ppermute(a, 'seq', down)  11 us
    pallas_call x4, Pallas kernels, attend_next(): pl.pallas_call(functools.partial(next_kernel, places=places), out_shape=o...  9.53 us
    ppermute x1, starting transfers between devices, body(): far_near = lax.ppermute(far, 'tp', other_core)  8.23 us
    psum x1, blocking collectives, body(): sums = lax.psum(stats, 'tp') / HQ  7.31 us
    ppermute x1, starting transfers between devices, body(): b1 = lax.ppermute(b, 'seq', up[0])  5.81 us
    unnamed x22, local copies, waits for them, and re-layouts  5.69 us
  transfers between devices with their start and end apart: 8, of which 3 were waited for; matrix products, arithmetic and copies ran while one was open for 0% of the time, Pallas kernels for 17%

profile of v5, /device:TPU:1, one launch (start us, length us, event | category | flops | bytes accessed | tf_op | source)
XLA Modules:
  0.0 114.3 jit_solution(2446158696057280811)
XLA Ops:
  0.0 4.8 %collective-permute-start = (bf16[1024,512]{1,0:T(8,128)(2,1)}, bf16[1024,512]{1,0:T(8,128)(2,1)S(1)}, u32[]{:S(2)}, u32[]{:S(2)}) collective-permute-start(bf16[1024,512]{1,0:T(8,128)(2,1)} %a_ref.1), channel_id=1, source_target_pairs={{0,2},{2,0},{1,3},{3,1},{4,6},{6,4},{5,7},{7,5},{8,10},{10,8},{9,1... | collective-permute-start | bytes 3145736 | tf_op jit(solution)/shard_map/ppermute | solution.py:265
  4.8 2.2 %shard_map.91 = (bf16[2,688,256]{2,1,0:T(8,128)(2,1)}, bf16[2,336,256]{2,1,0:T(8,128)(2,1)}) custom-call(bf16[1024,256]{1,0:T(8,128)(2,1)} %key_ref.3, bf16[1024,256]{1,0:T(8,128)(2,1)} %value_ref.3), custom_call_target="tpu_custom_call" | custom-call | tf_op jit(solution)/shard_map/pallas_call | solution.py:61
  7.0 5.8 %collective-permute-start.1 = (bf16[2,336,256]{2,1,0:T(8,128)(2,1)}, bf16[2,336,256]{2,1,0:T(8,128)(2,1)}, u32[]{:S(2)}, u32[]{:S(2)}) collective-permute-start(bf16[2,336,256]{2,1,0:T(8,128)(2,1)} %get-tuple-element.15), channel_id=1, source_target_pairs={{0,4},{4,8},{8,12},{12,0},{16,20},{20,24},{24,28},{28,16},{32,36},... | collective-permute-start | bytes 1032200 | tf_op jit(solution)/shard_map/ppermute | solution.py:267
  12.8 11.0 %collective-permute-start.6 = (bf16[2,688,256]{2,1,0:T(8,128)(2,1)}, bf16[2,688,256]{2,1,0:T(8,128)(2,1)}, u32[]{:S(2)}, u32[]{:S(2)}) collective-permute-start(bf16[2,688,256]{2,1,0:T(8,128)(2,1)} %get-tuple-element.20), channel_id=1, source_target_pairs={{0,508},{4,0},{8,4},{12,8},{16,12},{20,16},{24,20},{28,24},{32,28}... | collective-permute-start | bytes 2113544 | tf_op jit(solution)/shard_map/ppermute | solution.py:266
  23.8 3.1 %collective-permute-start.3 = (bf16[1024,512]{1,0:T(8,128)(2,1)}, bf16[1024,512]{1,0:T(8,128)(2,1)S(1)}, u32[]{:S(2)}, u32[]{:S(2)}) collective-permute-start(bf16[1024,512]{1,0:T(8,128)(2,1)} %a_ref.1), channel_id=1, source_target_pairs={{0,1},{1,0},{2,3},{3,2},{4,5},{5,4},{6,7},{7,6},{8,9},{9,8},{10,11... | collective-permute-start | bytes 3145736 | tf_op jit(solution)/shard_map/ppermute | solution.py:263
  27.0 23.3 %collective-permute-done.1 = bf16[2,336,256]{2,1,0:T(8,128)(2,1)} collective-permute-done((bf16[2,336,256]{2,1,0:T(8,128)(2,1)}, bf16[2,336,256]{2,1,0:T(8,128)(2,1)}, u32[]{:S(2)}, u32[]{:S(2)}) %collective-permute-start.1) | collective-permute-done | bytes 344096 | tf_op jit(solution)/shard_map/ppermute | solution.py:267
  50.3 2.7 %collective-permute-done.a_ref = bf16[1024,512]{1,0:T(8,128)(2,1)S(1)} collective-permute-done((bf16[1024,512]{1,0:T(8,128)(2,1)}, bf16[1024,512]{1,0:T(8,128)(2,1)S(1)}, u32[]{:S(2)}, u32[]{:S(2)}) %collective-permute-start) | collective-permute-done | bytes 1048608 | tf_op jit(solution)/shard_map/ppermute | solution.py:265
  53.0 8.2 %collective-permute-start.2 = (bf16[1024,512]{1,0:T(8,128)(2,1)S(1)}, bf16[1024,512]{1,0:T(8,128)(2,1)S(1)}, u32[]{:S(2)}, u32[]{:S(2)}) collective-permute-start(bf16[1024,512]{1,0:T(8,128)(2,1)S(1)} %collective-permute-done.a_ref), channel_id=1, source_target_pairs={{0,1},{1,0},{2,3},{3,2},{4,5},{5,4},{6,7},{7,6},{8,9},{9,8},{10,11... | collective-permute-start | bytes 3145736 | tf_op jit(solution)/shard_map/ppermute | solution.py:273
  61.2 1.9 %collective-permute-start.4 = (bf16[2,336,256]{2,1,0:T(8,128)(2,1)}, bf16[2,336,256]{2,1,0:T(8,128)(2,1)S(1)}, u32[]{:S(2)}, u32[]{:S(2)}) collective-permute-start(bf16[2,336,256]{2,1,0:T(8,128)(2,1)} %collective-permute-done.1), channel_id=1, source_target_pairs={{0,4},{4,504},{8,508},{12,0},{16,20},{20,8},{24,12},{28,16},{32,36... | collective-permute-start | bytes 1032200 | tf_op jit(solution)/shard_map/ppermute | solution.py:274
  63.2 0.0 collective-permute-done.6.refs_0_
  63.2 3.1 %collective-permute-start.7 = (bf16[2,688,256]{2,1,0:T(8,128)(2,1)}, bf16[2,688,256]{2,1,0:T(8,128)(2,1)}, u32[]{:S(2)}, u32[]{:S(2)}) collective-permute-start(bf16[2,688,256]{2,1,0:T(8,128)(2,1)} %collective-permute-done.6.refs_0_), channel_id=1, source_target_pairs={{0,508},{4,0},{8,4},{12,8},{16,12},{20,16},{24,20},{28,24},{32,28}... | collective-permute-start | bytes 2113544 | tf_op jit(solution)/shard_map/ppermute | solution.py:275
  66.3 0.1 pad_add_fusion.1.order_ref
  66.3 0.1 pad_add_fusion.order_ref
  66.4 12.1 %collective-permute-done.4.refs_0_ = bf16[2,336,256]{2,1,0:T(8,128)(2,1)S(1)} collective-permute-done((bf16[2,336,256]{2,1,0:T(8,128)(2,1)}, bf16[2,336,256]{2,1,0:T(8,128)(2,1)S(1)}, u32[]{:S(2)}, u32[]{:S(2)}) %collective-permute-start.4) | collective-permute-done | bytes 344096 | tf_op jit(solution)/shard_map/ppermute | solution.py:274
  78.5 2.7 %collective-permute-start.5 = (bf16[2,336,256]{2,1,0:T(8,128)(2,1)S(1)}, bf16[2,336,256]{2,1,0:T(8,128)(2,1)S(1)}, u32[]{:S(2)}, u32[]{:S(2)}) collective-permute-start(bf16[2,336,256]{2,1,0:T(8,128)(2,1)S(1)} %collective-permute-done.4.refs_0_), channel_id=1, source_target_pairs={{0,4},{4,8},{8,12},{12,16},{16,20},{20,24},{24,28},{28,32},{32,36}... | collective-permute-start | bytes 1032200 | tf_op jit(solution)/shard_map/ppermute | solution.py:278
  81.2 0.1 pad_add_fusion.2.seq_ref
  81.3 0.0 copy-start.7
  81.3 0.7 copy-done.7
  82.0 0.0 copy-start.8
  82.0 0.7 copy-done.8
  82.6 0.0 copy-start.9
  82.6 0.7 copy-done.9
  83.3 0.9 shard_map.94
  84.2 0.0 collective-permute-done.3.b_ref
  84.2 0.0 copy-start
  84.2 1.2 %copy-done = bf16[2048,256]{1,0:T(8,128)(2,1)S(1)} copy-done((bf16[2048,256]{1,0:T(8,128)(2,1)S(1)}, bf16[2048,256]{1,0:T(8,128)(2,1)}, u32[]{:S(2)}) %copy-start) | copy-done | bytes 1048600
  85.4 0.0 copy-start.2
  85.4 1.2 %copy-done.2 = bf16[2048,256]{1,0:T(8,128)(2,1)S(1)} copy-done((bf16[2048,256]{1,0:T(8,128)(2,1)S(1)}, bf16[2048,256]{1,0:T(8,128)(2,1)}, u32[]{:S(2)}) %copy-start.2) | copy-done | bytes 1048600
  86.6 0.0 copy-start.4
  86.6 1.2 %copy-done.4 = bf16[1024,512]{1,0:T(8,128)(2,1)S(1)} copy-done((bf16[1024,512]{1,0:T(8,128)(2,1)S(1)}, bf16[1024,512]{1,0:T(8,128)(2,1)}, u32[]{:S(2)}) %copy-start.4) | copy-done | bytes 1048600
  87.9 0.0 copy-start.1
  87.9 0.0 copy-start.3
  87.9 2.3 %shard_map.92.refs_0_ = f32[1024,512]{1,0:T(8,128)S(1)} custom-call(s32[2]{0:T(128)S(1)} %pad_add_fusion.1.order_ref, bf16[1024,512]{1,0:T(8,128)(2,1)S(1)} %copy-done.4, bf16[1024,512]{1,0:T(8,128)(2,1)S(1)} %collective-permute-done.3.b_ref, bf16[2048,256]{1,0:T(8,128)(2,1)S(1)} %copy-done, bf16[2048,256]{1,0:T(8,128)(2,1)S(1)} %copy-done, ...), custom_call_target="tpu_custom_call" | custom-call | flops 1073741824 | bytes 4194304 | tf_op jit(solution)/shard_map/pallas_call | solution.py:138
  90.2 0.0 copy-start.5
  90.2 0.0 copy-start.6
  90.2 0.0 collective-permute-done.2.b_ref
  90.3 0.0 copy-done.1
  90.3 0.0 copy-done.3
  90.3 2.4 %shard_map.93 = (bf16[1024,256]{1,0:T(8,128)(2,1)S(1)}, f32[1024,256]{1,0:T(8,128)S(1)}) custom-call(s32[2]{0:T(128)S(1)} %pad_add_fusion.order_ref, bf16[1024,512]{1,0:T(8,128)(2,1)S(1)} %collective-permute-done.a_ref, bf16[1024,512]{1,0:T(8,128)(2,1)S(1)} %collective-permute-done.2.b_ref, bf16[2048,256]{1,0:T(8,128)(2,1)S(1)} %copy-done.1, ...), custom_call_target="tpu_custom_call" | custom-call | flops 1073741824 | bytes 4194304 | tf_op jit(solution)/shard_map/pallas_call | solution.py:138
  92.7 0.0 copy-done.5
  92.7 0.0 copy-done.6
  92.7 3.5 %shard_map.95.refs_1_ = f32[1024,256]{1,0:T(8,128)S(1)} custom-call(bf16[1024,256]{1,0:T(8,128)(2,1)S(1)} %get-tuple-element.17.query_ref, s32[1024,128]{1,0:T(8,128)S(1)} %get-tuple-element.21.start_ref, s32[1024,128]{1,0:T(8,128)S(1)} %get-tuple-element.18.end_ref, bf16[1024,256]{1,0:T(8,128)(2,1)S(1)} %copy-done.5, bf16[1024,256]{1,0:T(8,128)(2,1)S(1)} %copy-done.6), custom_call_target="tpu_custom_call" | custom-call | flops 536870912 | bytes 2097152 | tf_op jit(solution)/shard_map/pallas_call | solution.py:212
  96.2 3.1 %shard_map.96.refs_1_ = f32[1024,256]{1,0:T(8,128)S(1)} custom-call(bf16[1024,256]{1,0:T(8,128)(2,1)S(1)} %get-tuple-element.17.query_ref, s32[1024,128]{1,0:T(8,128)S(1)} %get-tuple-element.18.end_ref, bf16[2,688,256]{2,1,0:T(8,128)(2,1)} %collective-permute-done.6.refs_0_, f32[1024,256]{1,0:T(8,128)S(1)} %shard_map.95.refs_1_), custom_call_target="tpu_custom_call", output_to_operand_aliasing={{}: (3, {})} | custom-call | flops 360710144 | bytes 2097152 | tf_op jit(solution)/shard_map/pallas_call | solution.py:228
  99.4 1.5 %shard_map.97.refs_1_ = f32[1024,256]{1,0:T(8,128)S(1)} custom-call(bf16[1024,256]{1,0:T(8,128)(2,1)S(1)} %get-tuple-element.17.query_ref, s32[1024,128]{1,0:T(8,128)S(1)} %get-tuple-element.18.end_ref, bf16[2,336,256]{2,1,0:T(8,128)(2,1)S(1)} %collective-permute-done.4.refs_0_, f32[1024,256]{1,0:T(8,128)S(1)} %shard_map.96.refs_1_), custom_call_target="tpu_custom_call", output_to_operand_aliasing={{}: (3, {})} | custom-call | flops 176160768 | bytes 2097152 | tf_op jit(solution)/shard_map/pallas_call | solution.py:228
  100.9 0.0 collective-permute-done.7.refs_0_
  100.9 3.1 %shard_map.98.refs_1_ = f32[1024,256]{1,0:T(8,128)S(1)} custom-call(bf16[1024,256]{1,0:T(8,128)(2,1)S(1)} %get-tuple-element.17.query_ref, s32[1024,128]{1,0:T(8,128)S(1)} %get-tuple-element.18.end_ref, bf16[2,688,256]{2,1,0:T(8,128)(2,1)} %collective-permute-done.7.refs_0_, f32[1024,256]{1,0:T(8,128)S(1)} %shard_map.97.refs_1_), custom_call_target="tpu_custom_call", output_to_operand_aliasing={{}: (3, {})} | custom-call | flops 360710144 | bytes 2097152 | tf_op jit(solution)/shard_map/pallas_call | solution.py:228
  104.0 0.0 copy-start.10
  104.0 0.0 collective-permute-done.5.refs_0_
  104.1 1.8 %shard_map.99 = (f32[1024,256]{1,0:T(8,128)S(1)}, f32[2,1024]{1,0:T(2,128)S(1)}) custom-call(bf16[1024,256]{1,0:T(8,128)(2,1)S(1)} %get-tuple-element.17.query_ref, s32[1024,128]{1,0:T(8,128)S(1)} %get-tuple-element.18.end_ref, bf16[2,336,256]{2,1,0:T(8,128)(2,1)S(1)} %collective-permute-done.5.refs_0_, ...), custom_call_target="tpu_custom_call", output_to_operand_aliasing={{0}: (3, {})} | custom-call | flops 176160768 | bytes 2097152 | tf_op jit(solution)/shard_map/pallas_call | solution.py:228
  105.8 7.3 %psum.7 = f32[2,1024]{1,0:T(2,128)S(1)} all-reduce(f32[2,1024]{1,0:T(2,128)S(1)} %get-tuple-element.23), channel_id=1, replica_groups=mesh['seq'=128,'tp'=4] {'tp'}, use_global_device_ids=true, to_apply=%region_0.0 | all-reduce | flops 2048 | bytes 16384 | tf_op jit(solution)/shard_map/psum | solution.py:285
  113.2 0.0 copy-done.10
  113.2 1.1 multiply_convert_fusion
  (3 shorter events, 0.0 us)
Async XLA Ops:
  0.0 53.0 %collective-permute-start = (bf16[1024,512]{1,0:T(8,128)(2,1)}, bf16[1024,512]{1,0:T(8,128)(2,1)S(1)}, u32[]{:S(2)}, u32[]{:S(2)}) collective-permute-start(bf16[1024,512]{1,0:T(8,128)(2,1)} %a_ref.1), channel_id=1, source_target_pairs={{0,2},{2,0},{1,3},{3,1},{4,6},{6,4},{5,7},{7,5},{8,10},{10,8},{9,1... | collective-permute-start | bytes 3145736 | tf_op jit(solution)/shard_map/ppermute | solution.py:265
  7.0 43.3 %collective-permute-start.1 = (bf16[2,336,256]{2,1,0:T(8,128)(2,1)}, bf16[2,336,256]{2,1,0:T(8,128)(2,1)}, u32[]{:S(2)}, u32[]{:S(2)}) collective-permute-start(bf16[2,336,256]{2,1,0:T(8,128)(2,1)} %get-tuple-element.15), channel_id=1, source_target_pairs={{0,4},{4,8},{8,12},{12,0},{16,20},{20,24},{24,28},{28,16},{32,36},... | collective-permute-start | bytes 1032200 | tf_op jit(solution)/shard_map/ppermute | solution.py:267
  12.8 50.3 %collective-permute-start.6 = (bf16[2,688,256]{2,1,0:T(8,128)(2,1)}, bf16[2,688,256]{2,1,0:T(8,128)(2,1)}, u32[]{:S(2)}, u32[]{:S(2)}) collective-permute-start(bf16[2,688,256]{2,1,0:T(8,128)(2,1)} %get-tuple-element.20), channel_id=1, source_target_pairs={{0,508},{4,0},{8,4},{12,8},{16,12},{20,16},{24,20},{28,24},{32,28}... | collective-permute-start | bytes 2113544 | tf_op jit(solution)/shard_map/ppermute | solution.py:266
  23.8 60.4 %collective-permute-start.3 = (bf16[1024,512]{1,0:T(8,128)(2,1)}, bf16[1024,512]{1,0:T(8,128)(2,1)S(1)}, u32[]{:S(2)}, u32[]{:S(2)}) collective-permute-start(bf16[1024,512]{1,0:T(8,128)(2,1)} %a_ref.1), channel_id=1, source_target_pairs={{0,1},{1,0},{2,3},{3,2},{4,5},{5,4},{6,7},{7,6},{8,9},{9,8},{10,11... | collective-permute-start | bytes 3145736 | tf_op jit(solution)/shard_map/ppermute | solution.py:263
  53.0 37.3 %collective-permute-start.2 = (bf16[1024,512]{1,0:T(8,128)(2,1)S(1)}, bf16[1024,512]{1,0:T(8,128)(2,1)S(1)}, u32[]{:S(2)}, u32[]{:S(2)}) collective-permute-start(bf16[1024,512]{1,0:T(8,128)(2,1)S(1)} %collective-permute-done.a_ref), channel_id=1, source_target_pairs={{0,1},{1,0},{2,3},{3,2},{4,5},{5,4},{6,7},{7,6},{8,9},{9,8},{10,11... | collective-permute-start | bytes 3145736 | tf_op jit(solution)/shard_map/ppermute | solution.py:273
  61.2 17.3 %collective-permute-start.4 = (bf16[2,336,256]{2,1,0:T(8,128)(2,1)}, bf16[2,336,256]{2,1,0:T(8,128)(2,1)S(1)}, u32[]{:S(2)}, u32[]{:S(2)}) collective-permute-start(bf16[2,336,256]{2,1,0:T(8,128)(2,1)} %collective-permute-done.1), channel_id=1, source_target_pairs={{0,4},{4,504},{8,508},{12,0},{16,20},{20,8},{24,12},{28,16},{32,36... | collective-permute-start | bytes 1032200 | tf_op jit(solution)/shard_map/ppermute | solution.py:274
  63.2 37.7 %collective-permute-start.7 = (bf16[2,688,256]{2,1,0:T(8,128)(2,1)}, bf16[2,688,256]{2,1,0:T(8,128)(2,1)}, u32[]{:S(2)}, u32[]{:S(2)}) collective-permute-start(bf16[2,688,256]{2,1,0:T(8,128)(2,1)} %collective-permute-done.6.refs_0_), channel_id=1, source_target_pairs={{0,508},{4,0},{8,4},{12,8},{16,12},{20,16},{24,20},{28,24},{32,28}... | collective-permute-start | bytes 2113544 | tf_op jit(solution)/shard_map/ppermute | solution.py:275
  78.5 25.5 %collective-permute-start.5 = (bf16[2,336,256]{2,1,0:T(8,128)(2,1)S(1)}, bf16[2,336,256]{2,1,0:T(8,128)(2,1)S(1)}, u32[]{:S(2)}, u32[]{:S(2)}) collective-permute-start(bf16[2,336,256]{2,1,0:T(8,128)(2,1)S(1)} %collective-permute-done.4.refs_0_), channel_id=1, source_target_pairs={{0,4},{4,8},{8,12},{12,16},{16,20},{20,24},{24,28},{28,32},{32,36}... | collective-permute-start | bytes 1032200 | tf_op jit(solution)/shard_map/ppermute | solution.py:278
  81.3 0.7 copy-start.7
  82.0 0.7 copy-start.8
  82.6 0.7 copy-start.9
  84.2 1.2 %copy-start = (bf16[2048,256]{1,0:T(8,128)(2,1)S(1)}, bf16[2048,256]{1,0:T(8,128)(2,1)}, u32[]{:S(2)}) copy-start(bf16[2048,256]{1,0:T(8,128)(2,1)} %wqb.3) | copy-start | bytes 3145732
  85.4 1.2 %copy-start.2 = (bf16[2048,256]{1,0:T(8,128)(2,1)S(1)}, bf16[2048,256]{1,0:T(8,128)(2,1)}, u32[]{:S(2)}) copy-start(bf16[2048,256]{1,0:T(8,128)(2,1)} %wgb.3) | copy-start | bytes 3145732
  86.6 1.2 %copy-start.4 = (bf16[1024,512]{1,0:T(8,128)(2,1)S(1)}, bf16[1024,512]{1,0:T(8,128)(2,1)}, u32[]{:S(2)}) copy-start(bf16[1024,512]{1,0:T(8,128)(2,1)} %a_ref.1) | copy-start | bytes 3145732
  87.9 2.4 %copy-start.1 = (bf16[2048,256]{1,0:T(8,128)(2,1)S(1)}, bf16[2048,256]{1,0:T(8,128)(2,1)}, u32[]{:S(2)}) copy-start(bf16[2048,256]{1,0:T(8,128)(2,1)} %wqb.3) | copy-start | bytes 3145732
  87.9 2.4 %copy-start.3 = (bf16[2048,256]{1,0:T(8,128)(2,1)S(1)}, bf16[2048,256]{1,0:T(8,128)(2,1)}, u32[]{:S(2)}) copy-start(bf16[2048,256]{1,0:T(8,128)(2,1)} %wgb.3) | copy-start | bytes 3145732
  90.2 2.5 %copy-start.5 = (bf16[1024,256]{1,0:T(8,128)(2,1)S(1)}, bf16[1024,256]{1,0:T(8,128)(2,1)}, u32[]{:S(2)}) copy-start(bf16[1024,256]{1,0:T(8,128)(2,1)} %key_ref.3) | copy-start | bytes 1572868
  90.2 2.5 %copy-start.6 = (bf16[1024,256]{1,0:T(8,128)(2,1)S(1)}, bf16[1024,256]{1,0:T(8,128)(2,1)}, u32[]{:S(2)}) copy-start(bf16[1024,256]{1,0:T(8,128)(2,1)} %value_ref.3) | copy-start | bytes 1572868
  104.0 9.2 %copy-start.10 = (f32[256]{0:T(256)S(1)}, f32[256]{0:T(256)}, u32[]{:S(2)}) copy-start(f32[256]{0:T(256)} %param.12) | copy-start | bytes 3076
